TPU v7x, 128 devices: a whole 4x4x4 slice. The times are simulated.
128 devices in a mesh: row: 8 (over z_lo, y), col: 16 (over x, z_hi, core).
Axes of the slice: x: 4, y: 4, z: 4 (z_hi: 2, z_lo: 2; z = z_hi * 2 + z_lo), core: 2. Of those that a mesh axis runs over, the one named last changes fastest.
Arguments:
- slab_rows: float32 [2048, 102400], P('row', 'col'), may hold values from -0.01953125 to 0.01953125
- slab_columns: float32 [102400, 2048], P('row', 'col'), may hold values from -0.125 to 0.125
- chol: float32 [64, 102400], P(None, 'col'), may hold values from -3 to 3
- pairs: int32 [2048], replicated, may hold values from 0 to 102399
Outputs:
- cycle_residual: float32 [2048, 102400], P('row', 'col')
All inputs are finite; a program needn't handle non-finite values.
Results may differ from a plain program's by a relative error of at most 0.000065.
Values sent between devices are 32-bit elements; how exact they have to be, the bound alone decides.
No kernel may reach another device: no remote copies, remote signals or barrier semaphores. Data moves between devices by JAX's collectives and lax.ppermute only.
A program may use at most 128 MiB of HBM per device.

v0:
```python
import jax
import jax.numpy as jnp
from jax import lax
from jax.sharding import PartitionSpec as P


def from_root(block, axis, owner):
    block = jnp.where(lax.axis_index(axis) == owner, block, jnp.zeros_like(block))
    return lax.psum(block, axis)


def body(slab_rows, slab_columns, chol, pairs):
    highest = lax.Precision.HIGHEST
    row_devices = lax.axis_size("row")
    col_devices = lax.axis_size("col")
    row_id = lax.axis_index("row")
    col_id = lax.axis_index("col")
    col_width = chol.shape[1]
    row_count = slab_rows.shape[0]
    slab_span = slab_columns.shape[1]
    local_index = pairs - col_id * col_width
    inside = (local_index >= 0) & (local_index < col_width)
    picked = (
        jnp.take(chol, jnp.clip(local_index, 0, col_width - 1), axis=1)
        * inside.astype(jnp.float32)[None, :]
    )
    slab_panel = lax.psum(picked, "col")
    own_panel = lax.dynamic_slice_in_dim(slab_panel, col_id * slab_span, slab_span, 1)
    mirror_part = lax.dot_general(
        own_panel,
        slab_columns,
        (((1,), (1,)), ((), ())),
        precision=highest,
        preferred_element_type=jnp.float32,
    )
    x_part = lax.dot_general(
        chol,
        slab_rows,
        (((1,), (1,)), ((), ())),
        precision=highest,
        preferred_element_type=jnp.float32,
    )
    x_full = lax.psum(x_part, "col")
    per_row = col_devices // row_devices
    summed = lax.psum(mirror_part, "col")
    own_half = lax.dynamic_slice_in_dim(summed, col_id % per_row * col_width, col_width, 1)
    mirror_cols = from_root(own_half, "row", col_id // per_row)
    rows_panel = lax.dynamic_slice_in_dim(slab_panel, row_id * row_count, row_count, 1)
    left_panel = jnp.concatenate([x_full, rows_panel], axis=0)
    right_panel = jnp.concatenate([chol, mirror_cols], axis=0)
    return lax.dot_general(
        left_panel,
        right_panel,
        (((0,), (0,)), ((), ())),
        precision=highest,
        preferred_element_type=jnp.float32,
    )


def solution(mesh):
    placed = (P("row", "col"), P("row", "col"), P(None, "col"), P())
    return jax.shard_map(
        body, mesh=mesh, in_specs=placed, out_specs=P("row", "col"), check_vma=False
    )
```

profile of v0, /device:TPU:0, one launch (start us, length us, event | category | flops | bytes accessed | tf_op | source)
XLA Modules:
  0.0 423.4 jit_solution(3352271313997981714)
XLA Ops:
  6.5 0.0 all-reduce.5.cloned.1.call-start
  6.5 0.7 fusion.9
  7.2 0.7 compare_and_fusion
  7.9 2.2 copy.5
  10.1 7.6 %gather_fusion = f32[2048,64]{1,0:T(8,128)} fusion(f32[64,6400]{0,1:T(8,128)S(1)} %copy.5, s32[2048]{0:T(1024)S(1)} %fusion.9), kind=kCustom, calls=%fused_computation | custom fusion | bytes 1056768 | tf_op jit(solution)/shard_map/jit(_take)/gather | solution.py:24
  17.8 0.0 copy-start
  17.8 2.6 multiply_bitcast_fusion
  20.4 0.0 all-reduce.5.cloned.1.call-update
  20.4 0.0 all-reduce.9.cloned.1.call-start
  20.5 0.0 copy-done
  20.5 7.9 %fusion.12 = f32[64,256]{0,1:T(8,128)} fusion(f32[64,6400]{1,0:T(8,128)S(1)} %copy-done, f32[256,6400]{1,0:T(8,128)} %param.4), kind=kOutput, calls=%fused_computation.19 | convolution fusion | flops 1258291200 | bytes 8257536 | tf_op jit(solution)/shard_map/dot_general | solution.py:36
  28.4 135.2 %all-reduce.5.cloned.1.call-done = f32[64,2048]{0,1:T(8,128)} async-done(((f32[64,2048]{0,1:T(8,128)}), f32[64,2048]{0,1:T(8,128)}) %all-reduce.5.cloned.1.call-update) | async-done | bytes 524304 | tf_op jit(solution)/shard_map/psum | solution.py:27
  163.6 10.2 %fusion.7 = f32[64,12800]{1,0:T(8,128)} fusion(f32[12800,128]{1,0:T(8,128)} %param.5, f32[64,2048]{0,1:T(8,128)} %all-reduce.5.cloned.1.call-done, s32[]{:T(128)S(6)} %select_n.42), kind=kOutput, calls=%fused_computation.10 | convolution fusion | flops 1258291200 | bytes 9895940 | tf_op jit(solution)/shard_map/dot_general | solution.py:29
  173.8 0.0 all-reduce.9.cloned.1.call-update
  173.9 0.0 all-reduce.7.cloned.1.call-start
  173.9 150.7 %all-reduce.9.cloned.1.call-done = (f32[64,12800]{1,0:T(8,128)}, f32[64,256]{0,1:T(8,128)}) async-done(((f32[64,12800]{1,0:T(8,128)}, f32[64,256]{0,1:T(8,128)}), (f32[64,12800]{1,0:T(8,128)}, f32[64,256]{0,1:T(8,128)})) %all-reduce.9.cloned.1.call-update) | async-done | bytes 3342352 | tf_op jit(solution)/shard_map/psum | solution.py:45
  324.6 0.0 copy-start.1
  324.6 2.7 dynamic-slice_select_fusion
  327.4 0.0 all-reduce.7.cloned.1.call-update
  327.4 0.9 constant_dynamic-slice_fusion
  328.3 79.5 %all-reduce.7.cloned.1.call-done = f32[64,6400]{1,0:T(8,128)} async-done(((f32[64,6400]{1,0:T(8,128)}), f32[64,6400]{1,0:T(8,128)}) %all-reduce.7.cloned.1.call-update) | async-done | bytes 1638416 | tf_op jit(solution)/shard_map/psum | solution.py:9
  407.8 0.0 copy-done.1
  407.8 9.1 %fusion = f32[256,6400]{1,0:T(8,128)} fusion(f32[64,6400]{1,0:T(8,128)} %all-reduce.7.cloned.1.call-done, f32[64,6400]{1,0:T(8,128)S(1)} %copy-done, f32[64,256]{0,1:T(8,128)S(1)} %constant_dynamic-slice_fusion, f32[64,256]{0,1:T(8,128)S(1)} %copy-done.1), kind=kOutput, calls=%fused_computation.1 | convolution fusion | flops 2517434368 | bytes 9961472 | tf_op jit(solution)/shard_map/dot_general | solution.py:51
Async XLA Ops:
  6.5 157.1 %all-reduce.5.cloned.1.call-start = ((), (), s32[]{:S(2)}) async-start(), calls=%async_computation | async-start | bytes 2097152 | tf_op jit(solution)/shard_map/psum | solution.py:27
  17.8 2.7 copy-start
  20.4 304.2 %all-reduce.9.cloned.1.call-start = ((), (), s32[]{:S(2)}) async-start(), calls=%async_computation.2 | async-start | bytes 6815744 | tf_op jit(solution)/shard_map/psum | solution.py:45
  173.9 234.0 %all-reduce.7.cloned.1.call-start = ((), (), s32[]{:S(2)}) async-start(), calls=%async_computation.1 | async-start | bytes 3276800 | tf_op jit(solution)/shard_map/psum | solution.py:9
  324.6 83.2 %copy-start.1 = (f32[64,256]{0,1:T(8,128)S(1)}, f32[64,256]{0,1:T(8,128)}, u32[]{:S(2)}) copy-start(f32[64,256]{0,1:T(8,128)} %get-tuple-element.6) | copy-start | bytes 196612
Sparse Core Ops, SparseCore 0:
  20.6 143.0 all-reduce.4
  174.0 150.6 all-reduce.8
  327.5 80.2 all-reduce.6
where the time goes:
time: 424 us; the launch traced here: 423 us
  waiting for transfers between devices  365 us (86%)
  matrix products  27.2 us (6%)
  between operations  13.2 us (3%)
  local copies, waits for them, and re-layouts  10.7 us (3%)
  other arithmetic  6.79 us (2%)
    psum x1, waiting for transfers between devices, body(): summed = lax.psum(mirror_part, 'col')  151 us
    psum x1, waiting for transfers between devices, body(): slab_panel = lax.psum(picked, 'col')  135 us
    psum x1, waiting for transfers between devices, from_root(): return lax.psum(block, axis)  79.5 us
    dot_general x1, matrix products, body(): lax.dot_general(own_panel, slab_columns, (((1,), (1,)), ((), ())), precis...  10.2 us
    dot_general x1, matrix products, body(): lax.dot_general(left_panel, right_panel, (((0,), (0,)), ((), ())), precis...  9.07 us
  transfers between devices with their start and end apart: 3, of which 3 were waited for; matrix products, arithmetic and copies ran while one was open for 2% of the time, Pallas kernels for 0%

commit v1 on v0

v1 whole, which is shorter than its diff:
```python
import jax
import jax.numpy as jnp
import numpy as np
from jax import lax
from jax.experimental import pallas as pl
from jax.experimental.pallas import tpu as pltpu
from jax.sharding import PartitionSpec as P

SLOT = np.array(
    [
        [2, 4, 1, 5, 0, 6, 3, 7],
        [6, 2, 4, 7, 3, 1, 5, 0],
        [4, 7, 5, 1, 6, 3, 0, 2],
        [7, 5, 2, 3, 6, 4, 0, 1],
        [6, 1, 4, 3, 7, 5, 2, 0],
        [1, 0, 2, 6, 5, 7, 4, 3],
        [5, 3, 6, 2, 4, 1, 7, 0],
        [2, 1, 5, 7, 3, 0, 4, 6],
    ],
    np.int32,
)
CORE = [(d, d ^ 1) for d in range(128)]
TURN = [(r * 16 + c, int(SLOT[r, c // 2]) * 16 + 2 * r + c % 2) for r in range(8) for c in range(16)]
PLANE = [[2 * j + k for j in range(8)] for k in range(2)]
BOTH = ("row", "col")


def gather_kernel(index_ref, chol_ref, out_ref):
    groups = chol_ref.shape[0] // 8
    tiles = chol_ref.shape[1] // 128

    def piece(s, _):
        index = index_ref[pl.ds(s, 1), :]
        index = jnp.broadcast_to(index, (8, 128))
        lane = index & 127
        tile = index >> 7

        def step(t, accs):
            hit = tile == t
            start = pl.multiple_of(t * 128, 128)
            new = []
            for g in range(groups):
                block = chol_ref[g * 8 : g * 8 + 8, pl.ds(start, 128)]
                new.append(jnp.where(hit, jnp.take_along_axis(block, lane, axis=1), accs[g]))
            return tuple(new)

        zero = jnp.zeros((8, 128), jnp.float32)
        accs = lax.fori_loop(0, tiles, step, (zero,) * groups, unroll=5)
        for g in range(groups):
            out_ref[s, g * 8 : g * 8 + 8, :] = accs[g]
        return 0

    lax.fori_loop(0, index_ref.shape[0], piece, 0)


def gather(chol, index):
    pieces = index.shape[0]
    return pl.pallas_call(
        gather_kernel,
        out_shape=jax.ShapeDtypeStruct((pieces, chol.shape[0], 128), jnp.float32),
        in_specs=[pl.BlockSpec(memory_space=pltpu.VMEM)] * 2,
        out_specs=pl.BlockSpec(memory_space=pltpu.VMEM),
        compiler_params=pltpu.CompilerParams(vmem_limit_bytes=16 * 1024 * 1024),
    )(index, chol)


def dot(a, b, dims):
    return lax.dot_general(
        a, b, (dims, ((), ())), precision=lax.Precision.HIGH, preferred_element_type=jnp.float32
    )


def body(slab_rows, slab_columns, chol, pairs):
    row_id = lax.axis_index("row")
    col_id = lax.axis_index("col")
    core = col_id % 2
    nchol, width = chol.shape
    count = slab_rows.shape[0]

    index = pairs.reshape(16, 128) - col_id * width
    picked = gather(chol, index)
    own = jnp.sum(lax.all_to_all(picked, "col", 0, 0), axis=0)

    order = jnp.asarray(SLOT)[row_id]
    turned = own.reshape(8, 8, 128)[order].reshape(nchol, 128)
    x_part = dot(chol, slab_rows, ((1,), (1,)))
    theirs = lax.dynamic_slice_in_dim(slab_columns, (1 - core) * width, width, 0)
    mine = lax.dynamic_slice_in_dim(slab_columns, core * width, width, 0)
    m_theirs = jnp.concatenate([dot(turned, theirs, ((1,), (1,))), x_part], axis=1)
    got = lax.ppermute(m_theirs, BOTH, CORE)
    m_mine = jnp.concatenate([dot(turned, mine, ((1,), (1,))), x_part], axis=1) + got

    pieces = lax.all_to_all(m_mine.reshape(8, 8, width + count), "col", 0, 0, axis_index_groups=PLANE)
    summed = jnp.sum(pieces, axis=0)
    sent = lax.ppermute(summed[:, :width], BOTH, TURN)

    other = lax.ppermute(own, BOTH, CORE)
    x_slice = summed[:, width:].reshape(8, 2, 128).transpose(1, 0, 2).reshape(16, 128)
    small = jnp.concatenate([x_slice, jnp.where(core == 0, own, other), jnp.where(core == 0, other, own)], axis=0)
    small = lax.all_to_all(jnp.broadcast_to(small, (8,) + small.shape), "col", 0, 0, axis_index_groups=PLANE)
    x_full = small[:, :16].reshape(8, 2, 8, 128).transpose(0, 2, 1, 3).reshape(nchol, count)
    rows = lax.dynamic_index_in_dim(small, row_id, 0, keepdims=False)[16:]
    rows = rows.reshape(2, nchol, 128).transpose(1, 0, 2).reshape(nchol, count)
    left = jnp.concatenate([x_full, rows], axis=0)

    mirrored = lax.all_to_all(jnp.broadcast_to(sent, (8,) + sent.shape), "row", 0, 0).reshape(nchol, width)
    return dot(left, jnp.concatenate([chol, mirrored], axis=0), ((0,), (0,)))


def solution(mesh):
    placed = (P("row", "col"), P("row", "col"), P(None, "col"), P())
    return jax.shard_map(
        body, mesh=mesh, in_specs=placed, out_specs=P("row", "col"), check_vma=False
    )
```

time: 424 us -> 143 us (0.34)
  waiting for transfers between devices: 365 us -> 63.5 us
  starting transfers between devices: 0.09 us -> 29.1 us
  Pallas kernels: 0 us -> 18.8 us
  between operations: 13.2 us -> 0.11 us
  matrix products: 27.2 us -> 18.3 us
  local copies, waits for them, and re-layouts: 10.7 us -> 5.92 us
    psum x3 -> x0, waiting for transfers between devices: 365 us -> none  [the longest x1 151 us: body(): summed = lax.psum(mirror_part, 'col')]
    all_to_all x0 -> x4, waiting for transfers between devices: none -> 53.3 us  [the longest x1 25 us: body(): lax.all_to_all(m_mine.reshape(8, 8, width + count), 'col', 0, 0, axis_ind...]
    all_to_all x0 -> x4, starting transfers between devices: none -> 23.4 us  [the longest x1 7.8 us: body(): lax.all_to_all(jnp.broadcast_to(sent, (8,) + sent.shape), 'row', 0, 0)]
    pallas_call x0 -> x1, Pallas kernels: none -> 18.8 us  [gather(): pl.pallas_call(gather_kernel, out_shape=jax.ShapeDtypeStruct((pieces, cho...]
    ppermute x0 -> x3, waiting for transfers between devices: none -> 10.2 us  [the longest x1 9.31 us: body(): sent = lax.ppermute(summed[:, :width], BOTH, TURN)]
    dot_general x3 -> x4, matrix products: 27.2 us -> 18.3 us  [dot(): lax.dot_general(a, b, (dims, ((), ())), precision=lax.Precision.HIGH, pre...]
    gather x1, local copies, waits for them, and re-layouts: 7.64 us -> 0.55 us  [body(): turned = own.reshape(8, 8, 128)[order].reshape(nchol, 128)]
    ppermute x0 -> x3, starting transfers between devices: none -> 5.67 us  [the longest x1 5.11 us: body(): sent = lax.ppermute(summed[:, :width], BOTH, TURN)]
  transfers between devices with their start and end apart: 3 -> 7, of which waited for: 3 -> 6; matrix products, arithmetic and copies ran while one was open for 2% -> 9% of each run, Pallas kernels for 0% -> 0%
where the time goes in v1:
time: 143 us; the launch traced here: 141 us
  waiting for transfers between devices  63.5 us (44%)
  starting transfers between devices  29.1 us (20%)
  Pallas kernels  18.8 us (13%)
  matrix products  18.3 us (13%)
  local copies, waits for them, and re-layouts  5.92 us (4%)
  other arithmetic  5.65 us (4%)
    all_to_all x1, waiting for transfers between devices, body(): lax.all_to_all(m_mine.reshape(8, 8, width + count), 'col', 0, 0, axis_ind...  25 us
    all_to_all x1, waiting for transfers between devices, body(): lax.all_to_all(jnp.broadcast_to(sent, (8,) + sent.shape), 'row', 0, 0)  20 us
    pallas_call x1, Pallas kernels, gather(): pl.pallas_call(gather_kernel, out_shape=jax.ShapeDtypeStruct((pieces, cho...  18.8 us
    dot_general x4, matrix products, dot(): lax.dot_general(a, b, (dims, ((), ())), precision=lax.Precision.HIGH, pre...  18.3 us
    ppermute x1, waiting for transfers between devices, body(): sent = lax.ppermute(summed[:, :width], BOTH, TURN)  9.31 us
    all_to_all x1, starting transfers between devices, body(): lax.all_to_all(jnp.broadcast_to(sent, (8,) + sent.shape), 'row', 0, 0)  7.8 us
    all_to_all x1, starting transfers between devices, body(): own = jnp.sum(lax.all_to_all(picked, 'col', 0, 0), axis=0)  7.8 us
    all_to_all x1, waiting for transfers between devices, body(): own = jnp.sum(lax.all_to_all(picked, 'col', 0, 0), axis=0)  5.63 us
  transfers between devices with their start and end apart: 7, of which 6 were waited for; matrix products, arithmetic and copies ran while one was open for 9% of the time, Pallas kernels for 0%

profile of v1, /device:TPU:0, one launch (start us, length us, event | category | flops | bytes accessed | tf_op | source)
XLA Modules:
  0.0 141.3 jit_solution(12369089291525072866)
XLA Ops:
  0.0 0.7 subtract_bitcast_fusion.index_ref
  0.7 0.0 copy-start
  0.7 1.4 %copy-done = f32[64,6400]{1,0:T(8,128)S(1)} copy-done((f32[64,6400]{1,0:T(8,128)S(1)}, f32[64,6400]{1,0:T(8,128)}, u32[]{:S(2)}) %copy-start) | copy-done | bytes 1638424
  2.1 0.0 copy-start.1
  2.1 18.8 %shard_map.55 = f32[16,64,128]{2,1,0:T(8,128)} custom-call(s32[16,128]{1,0:T(8,128)S(1)} %subtract_bitcast_fusion.index_ref, f32[64,6400]{1,0:T(8,128)S(1)} %copy-done), custom_call_target="tpu_custom_call" | custom-call | tf_op jit(solution)/shard_map/pallas_call | solution.py:58
  20.9 7.8 %all-to-all-start = ((f32[16,64,128]{2,1,0:T(8,128)}), f32[16,64,128]{2,1,0:T(8,128)S(1)}, u32[]{:S(2)}, u32[]{:S(2)}) async-start(f32[16,64,128]{2,1,0:T(8,128)} %shard_map.55), calls=%async_computation | async-start | bytes 1048576 | tf_op jit(solution)/shard_map/all_to_all | solution.py:82
  28.7 0.7 fusion.18
  29.4 0.0 copy-done.1
  29.4 6.0 %fusion.20 = f32[64,256]{1,0:T(8,128)S(1)} fusion(f32[64,6400]{1,0:T(8,128)S(1)} %copy-done.1, f32[256,6400]{1,0:T(8,128)} %param.5), kind=kOutput, calls=%fused_computation.34 | convolution fusion | flops 629145600 | bytes 8257536 | tf_op jit(solution)/shard_map/dot_general | solution.py:68
  35.4 5.6 %all-to-all-done = f32[16,64,128]{2,1,0:T(8,128)S(1)} async-done(((f32[16,64,128]{2,1,0:T(8,128)}), f32[16,64,128]{2,1,0:T(8,128)S(1)}, u32[]{:S(2)}, u32[]{:S(2)}) %all-to-all-start) | async-done | bytes 524320 | tf_op jit(solution)/shard_map/all_to_all | solution.py:82
  41.1 0.6 gather_fusion
  41.7 3.8 %fusion.4 = f32[64,6400]{1,0:T(8,128)S(1)} fusion(f32[12800,128]{1,0:T(8,128)} %param.6, s32[]{:T(128)S(6)} %select_n.44, f32[8,8,128]{2,1,0:T(8,128)S(1)} %gather_fusion), kind=kOutput, calls=%fused_computation.5 | convolution fusion | flops 314572800 | bytes 4947972 | tf_op jit(solution)/shard_map/dot_general | solution.py:68
  45.4 1.3 pad_maximum_fusion
  46.7 0.0 collective-permute-start
  46.7 3.8 %fusion.6 = f32[64,6400]{1,0:T(8,128)S(1)} fusion(f32[12800,128]{1,0:T(8,128)} %param.6, s32[]{:T(128)S(6)} %select_n.43, f32[8,8,128]{2,1,0:T(8,128)S(1)} %gather_fusion), kind=kOutput, calls=%fused_computation.7 | convolution fusion | flops 314572800 | bytes 4947972 | tf_op jit(solution)/shard_map/dot_general | solution.py:68
  50.5 0.0 collective-permute-done
  50.5 1.4 %fusion.9 = f32[8,8,6656]{2,1,0:T(8,128)} fusion(f32[64,6656]{1,0:T(8,128)S(1)} %collective-permute-done, f32[64,256]{1,0:T(8,128)S(1)} %fusion.20, f32[64,6400]{1,0:T(8,128)S(1)} %fusion.6), kind=kLoop, calls=%fused_computation.12 | loop fusion | flops 851968 | bytes 5111808 | tf_op jit(solution)/shard_map/reshape | solution.py:93
  52.0 3.6 %all-to-all-start.1 = ((f32[8,8,6656]{2,1,0:T(8,128)}), f32[8,8,6656]{2,1,0:T(8,128)S(1)}, u32[]{:S(2)}, u32[]{:S(2)}) async-start(f32[8,8,6656]{2,1,0:T(8,128)} %fusion.9), calls=%async_computation.1 | async-start | bytes 3407872 | tf_op jit(solution)/shard_map/all_to_all | solution.py:93
  55.5 0.6 collective-permute-start.1
  56.1 0.9 collective-permute-done.1
  57.0 0.6 broadcast_select_fusion.1
  57.6 25.0 %all-to-all-done.1 = f32[8,8,6656]{2,1,0:T(8,128)S(1)} async-done(((f32[8,8,6656]{2,1,0:T(8,128)}), f32[8,8,6656]{2,1,0:T(8,128)S(1)}, u32[]{:S(2)}, u32[]{:S(2)}) %all-to-all-start.1) | async-done | bytes 1703968 | tf_op jit(solution)/shard_map/all_to_all | solution.py:93
  82.6 0.1 reduce_sum.19
  82.7 0.8 pad_maximum_fusion.2
  83.5 0.9 broadcast_in_dim.7
  84.3 4.2 %all-to-all-start.2 = ((f32[8,144,128]{2,1,0:T(8,128)}), f32[8,144,128]{2,1,0:T(8,128)S(1)}, u32[]{:S(2)}, u32[]{:S(2)}) async-start(f32[8,144,128]{2,1,0:T(8,128)} %broadcast_in_dim.7), calls=%async_computation.2 | async-start | bytes 1179648 | tf_op jit(solution)/shard_map/all_to_all | solution.py:100
  88.6 5.1 %collective-permute-start.2 = (f32[8,6400]{1,0:T(8,128)S(1)}, f32[8,6400]{1,0:T(8,128)S(1)}, u32[]{:S(2)}, u32[]{:S(2)}) collective-permute-start(f32[8,6400]{1,0:T(8,128)S(1)} %slice.21), channel_id=1, source_target_pairs={{0,32},{1,33},{2,64},{3,65},{4,16},{5,17},{6,80},{7,81},{8,0},{9,1... | collective-permute-start | bytes 614408 | tf_op jit(solution)/shard_map/ppermute | solution.py:95
  93.7 9.3 %collective-permute-done.2 = f32[8,6400]{1,0:T(8,128)S(1)} collective-permute-done((f32[8,6400]{1,0:T(8,128)S(1)}, f32[8,6400]{1,0:T(8,128)S(1)}, u32[]{:S(2)}, u32[]{:S(2)}) %collective-permute-start.2) | collective-permute-done | bytes 204832 | tf_op jit(solution)/shard_map/ppermute | solution.py:95
  103.0 2.7 %all-to-all-done.2 = f32[8,144,128]{2,1,0:T(8,128)S(1)} async-done(((f32[8,144,128]{2,1,0:T(8,128)}), f32[8,144,128]{2,1,0:T(8,128)S(1)}, u32[]{:S(2)}, u32[]{:S(2)}) %all-to-all-start.2) | async-done | bytes 589856 | tf_op jit(solution)/shard_map/all_to_all | solution.py:100
  105.7 0.0 copy-start.2
  105.7 1.4 broadcast_in_dim.8
  107.0 0.0 copy-done.2
  107.0 7.8 %all-to-all-start.3 = ((f32[8,8,6400]{2,1,0:T(8,128)}), f32[8,8,6400]{2,1,0:T(8,128)S(1)}, u32[]{:S(2)}, u32[]{:S(2)}) async-start(f32[8,8,6400]{2,1,0:T(8,128)} %broadcast_in_dim.8), calls=%async_computation.3 | async-start | bytes 3276800 | tf_op jit(solution)/shard_map/all_to_all | solution.py:106
  114.8 0.8 constant_dynamic-slice_fusion
  115.7 0.8 slice_bitcast_fusion
  116.6 20.0 %all-to-all-done.3 = f32[8,8,6400]{2,1,0:T(8,128)S(1)} async-done(((f32[8,8,6400]{2,1,0:T(8,128)}), f32[8,8,6400]{2,1,0:T(8,128)S(1)}, u32[]{:S(2)}, u32[]{:S(2)}) %all-to-all-start.3) | async-done | bytes 1638432 | tf_op jit(solution)/shard_map/all_to_all | solution.py:106
  136.6 4.7 %fusion = f32[256,6400]{1,0:T(8,128)} fusion(f32[64,6400]{1,0:T(8,128)S(1)} %bitcast.40, f32[64,6400]{1,0:T(8,128)S(1)} %copy-done.1, f32[64,256]{1,0:T(8,128)S(1)} %bitcast.42, f32[64,256]{1,0:T(8,128)S(1)} %slice_bitcast_fusion), kind=kOutput, calls=%fused_computation.1 | convolution fusion | flops 1259143168 | bytes 9961472 | tf_op jit(solution)/shard_map/dot_general | solution.py:68
  (5 shorter events, 0.1 us)
Async XLA Ops:
  0.7 1.4 %copy-start = (f32[64,6400]{1,0:T(8,128)S(1)}, f32[64,6400]{1,0:T(8,128)}, u32[]{:S(2)}) copy-start(f32[64,6400]{1,0:T(8,128)} %chol_ref.1) | copy-start | bytes 4915204
  2.1 27.3 %copy-start.1 = (f32[64,6400]{1,0:T(8,128)S(1)}, f32[64,6400]{1,0:T(8,128)}, u32[]{:S(2)}) copy-start(f32[64,6400]{1,0:T(8,128)} %chol_ref.1) | copy-start | bytes 4915204
  20.9 20.2 %all-to-all-start = ((f32[16,64,128]{2,1,0:T(8,128)}), f32[16,64,128]{2,1,0:T(8,128)S(1)}, u32[]{:S(2)}, u32[]{:S(2)}) async-start(f32[16,64,128]{2,1,0:T(8,128)} %shard_map.55), calls=%async_computation | async-start | bytes 1048576 | tf_op jit(solution)/shard_map/all_to_all | solution.py:82
  46.7 3.8 %collective-permute-start = (f32[64,6656]{1,0:T(8,128)}, f32[64,6656]{1,0:T(8,128)S(1)}, u32[]{:S(2)}, u32[]{:S(2)}) collective-permute-start(f32[64,6656]{1,0:T(8,128)} %pad_maximum_fusion), channel_id=1, source_target_pairs={{0,1},{1,0},{2,3},{3,2},{4,5},{5,4},{6,7},{7,6},{8,9},{9,8},{10,11... | collective-permute-start | bytes 5111816 | tf_op jit(solution)/shard_map/ppermute | solution.py:90
  52.0 30.6 %all-to-all-start.1 = ((f32[8,8,6656]{2,1,0:T(8,128)}), f32[8,8,6656]{2,1,0:T(8,128)S(1)}, u32[]{:S(2)}, u32[]{:S(2)}) async-start(f32[8,8,6656]{2,1,0:T(8,128)} %fusion.9), calls=%async_computation.1 | async-start | bytes 3407872 | tf_op jit(solution)/shard_map/all_to_all | solution.py:93
  55.5 1.4 %collective-permute-start.1 = (f32[64,128]{1,0:T(8,128)S(1)}, f32[64,128]{1,0:T(8,128)S(1)}, u32[]{:S(2)}, u32[]{:S(2)}) collective-permute-start(f32[64,128]{1,0:T(8,128)S(1)} %reduce_sum.18), channel_id=1, source_target_pairs={{0,1},{1,0},{2,3},{3,2},{4,5},{5,4},{6,7},{7,6},{8,9},{9,8},{10,11... | collective-permute-start | bytes 98312 | tf_op jit(solution)/shard_map/ppermute | solution.py:97
  84.3 21.4 %all-to-all-start.2 = ((f32[8,144,128]{2,1,0:T(8,128)}), f32[8,144,128]{2,1,0:T(8,128)S(1)}, u32[]{:S(2)}, u32[]{:S(2)}) async-start(f32[8,144,128]{2,1,0:T(8,128)} %broadcast_in_dim.7), calls=%async_computation.2 | async-start | bytes 1179648 | tf_op jit(solution)/shard_map/all_to_all | solution.py:100
  88.6 14.4 %collective-permute-start.2 = (f32[8,6400]{1,0:T(8,128)S(1)}, f32[8,6400]{1,0:T(8,128)S(1)}, u32[]{:S(2)}, u32[]{:S(2)}) collective-permute-start(f32[8,6400]{1,0:T(8,128)S(1)} %slice.21), channel_id=1, source_target_pairs={{0,32},{1,33},{2,64},{3,65},{4,16},{5,17},{6,80},{7,81},{8,0},{9,1... | collective-permute-start | bytes 614408 | tf_op jit(solution)/shard_map/ppermute | solution.py:95
  105.7 1.4 copy-start.2
  107.0 29.5 %all-to-all-start.3 = ((f32[8,8,6400]{2,1,0:T(8,128)}), f32[8,8,6400]{2,1,0:T(8,128)S(1)}, u32[]{:S(2)}, u32[]{:S(2)}) async-start(f32[8,8,6400]{2,1,0:T(8,128)} %broadcast_in_dim.8), calls=%async_computation.3 | async-start | bytes 3276800 | tf_op jit(solution)/shard_map/all_to_all | solution.py:106

commit v2 on v1

v2 whole, which is shorter than its diff:
```python
import jax
import jax.numpy as jnp
import numpy as np
from jax import lax
from jax.experimental import pallas as pl
from jax.experimental.pallas import tpu as pltpu
from jax.sharding import PartitionSpec as P

F32, BF16 = jnp.float32, jnp.bfloat16
MIB = 1024 * 1024
BOTH = ("row", "col")

SLOT = np.array(
    [
        [2, 4, 1, 5, 0, 6, 3, 7],
        [6, 2, 4, 7, 3, 1, 5, 0],
        [4, 7, 5, 1, 6, 3, 0, 2],
        [7, 5, 2, 3, 6, 4, 0, 1],
        [6, 1, 4, 3, 7, 5, 2, 0],
        [1, 0, 2, 6, 5, 7, 4, 3],
        [5, 3, 6, 2, 4, 1, 7, 0],
        [2, 1, 5, 7, 3, 0, 4, 6],
    ],
    np.int32,
)
CODE = [sum(int(v) << (3 * j) for j, v in enumerate(line)) for line in SLOT]
PLANE = [[2 * j + k for j in range(8)] for k in range(2)]


def moves(to):
    return [(r * 16 + c, (lambda d: d[0] * 16 + d[1])(to(r, c))) for r in range(8) for c in range(16)]


CORE = moves(lambda r, c: (r, c ^ 1))
ZPAIR = moves(lambda r, c: (r ^ 4, c))
TURN = moves(lambda r, c: (int(SLOT[r, c // 2]), 2 * r + c % 2))
FLIP = moves(lambda r, c: (c // 2, 2 * r + c % 2))

VMEM = pl.BlockSpec(memory_space=pltpu.VMEM)
ANY = pl.BlockSpec(memory_space=pl.ANY)


def split(x):
    hi = x.astype(BF16)
    return hi, (x - hi.astype(F32)).astype(BF16)


def nt(a, b):
    return lax.dot_general(a, b, (((1,), (1,)), ((), ())), preferred_element_type=F32)


def nn(a, b):
    return lax.dot_general(a, b, (((1,), (0,)), ((), ())), preferred_element_type=F32)


def pick_kernel(pairs_ref, chol_ref, out_ref, held_ref, sem):
    width = chol_ref.shape[1]
    tiles = width // 128
    half = held_ref.shape[0]
    start = pl.multiple_of(lax.axis_index("row") // 4 * half, half)
    copy = pltpu.make_async_copy(chol_ref.at[pl.ds(start, half), :], held_ref, sem)
    copy.start()
    base = lax.axis_index("col") * width
    lanes = lax.broadcasted_iota(jnp.int32, (128, 128), 0)
    copy.wait()
    stack = jnp.concatenate([held_ref[:, t * 128 : t * 128 + 128] for t in range(tiles)], axis=0)
    stack = jnp.concatenate(split(stack), axis=1)
    for s in range(0, out_ref.shape[0], 2):
        index = [pairs_ref[s + i : s + i + 1, :] - base for i in range(2)]
        hot = jnp.concatenate([jnp.where(lanes == (i & 127), 1.0, 0.0) for i in index], axis=1).astype(BF16)
        found = nn(stack, jnp.concatenate([hot, hot], axis=0))
        tile = jnp.broadcast_to(jnp.concatenate([i >> 7 for i in index], axis=1), (half, 256))
        total = jnp.zeros((half, 256), F32)
        for t in range(tiles):
            total = jnp.where(tile == t, found[t * half : t * half + half], total)
        out_ref[s] = total[:, :128]
        out_ref[s + 1] = total[:, 128:]


def pick(pairs, chol):
    half = chol.shape[0] // 2
    return pl.pallas_call(
        pick_kernel,
        out_shape=jax.ShapeDtypeStruct((pairs.shape[0], half, 128), F32),
        in_specs=[VMEM, ANY],
        out_specs=VMEM,
        scratch_shapes=[pltpu.VMEM((half, chol.shape[1]), F32), pltpu.SemaphoreType.DMA],
        compiler_params=pltpu.CompilerParams(vmem_limit_bytes=56 * MIB),
    )(pairs, chol)


def prepare_kernel(u_ref, out_ref):
    hi, lo = split(u_ref[...].T)
    out_ref[:128, :] = hi
    out_ref[128:, :] = lo


def prepare(u, tile=3200):
    count, span = u.shape
    return pl.pallas_call(
        prepare_kernel,
        out_shape=jax.ShapeDtypeStruct((2 * span, count), BF16),
        grid=(count // tile,),
        in_specs=[pl.BlockSpec((tile, span), lambda k: (k, 0))],
        out_specs=pl.BlockSpec((2 * span, tile), lambda k: (0, k)),
        compiler_params=pltpu.CompilerParams(vmem_limit_bytes=40 * MIB),
        cost_estimate=pl.CostEstimate(flops=0, bytes_accessed=13 * MIB, transcendentals=0),
    )(u)


def contract_kernel(chol_ref, rows_ref, x_ref):
    @pl.when(pl.program_id(0) == 0)
    def _():
        x_ref[...] = jnp.zeros_like(x_ref)

    nchol = chol_ref.shape[0]
    a_hi, a_lo = split(chol_ref[...])
    b_hi, b_lo = split(rows_ref[...])
    both = nt(jnp.concatenate([a_hi, a_lo], axis=0), b_hi)
    x_ref[...] += both[:nchol] + both[nchol:] + nt(a_hi, b_lo)


def contract(chol, rows, tile=3200):
    nchol, width = chol.shape
    count = rows.shape[0]
    return pl.pallas_call(
        contract_kernel,
        out_shape=jax.ShapeDtypeStruct((nchol, count), F32),
        grid=(width // tile,),
        in_specs=[pl.BlockSpec((nchol, tile), lambda k: (0, k)), pl.BlockSpec((count, tile), lambda k: (0, k))],
        out_specs=pl.BlockSpec((nchol, count), lambda k: (0, 0)),
        compiler_params=pltpu.CompilerParams(vmem_limit_bytes=56 * MIB),
        cost_estimate=pl.CostEstimate(
            flops=6 * nchol * width * count, bytes_accessed=4 * width * (nchol + count), transcendentals=0
        ),
    )(chol, rows)


def mirror_kernel(mine, own_ref, other_ref, u_ref, out_ref):
    width = out_ref.shape[1]
    core = lax.rem(lax.axis_index("col"), 2)
    start = pl.multiple_of((core if mine else 1 - core) * width, 128)
    row = lax.axis_index("row")
    code = jnp.int32(CODE[0])
    for r in range(1, 8):
        code = jnp.where(row == r, jnp.int32(CODE[r]), code)
    slices = []
    for j in range(8):
        at = (code >> (3 * j)) & 7
        rows = pl.ds(pl.multiple_of((at & 3) * 8, 8), 8)
        slices.append(jnp.where((at >> 2) == (row >> 2), own_ref[rows, :], other_ref[rows, :]))
    hi, lo = split(jnp.concatenate(slices, axis=0))
    top = jnp.concatenate([hi, hi], axis=1)
    low = jnp.concatenate([lo, jnp.zeros_like(lo)], axis=1)
    both = nn(jnp.concatenate([top, low], axis=0), u_ref[:, pl.ds(start, width)])
    out_ref[...] = both[:64] + both[64:]


def mirror(mine, own, other, u):
    width = u.shape[1] // 2
    return pl.pallas_call(
        lambda *refs: mirror_kernel(mine, *refs),
        out_shape=jax.ShapeDtypeStruct((64, width), F32),
        in_specs=[VMEM] * 3,
        out_specs=VMEM,
        compiler_params=pltpu.CompilerParams(vmem_limit_bytes=30 * MIB),
        cost_estimate=pl.CostEstimate(flops=6 * 64 * 128 * width, bytes_accessed=5 * MIB, transcendentals=0),
    )(own, other, u)


def final_kernel(x_ref, rows_ref, chol_ref, m_ref, out_ref, held, sems):
    tile = held.shape[2]
    left = jnp.concatenate([x_ref[...], jnp.concatenate([rows_ref[0], rows_ref[1]], axis=1)], axis=0).T
    left = jnp.concatenate(split(left), axis=1)
    copies = []
    for k in range(held.shape[0]):
        here = slice(k * tile, k * tile + tile)
        r_hi, r_lo = split(jnp.concatenate([chol_ref[:, here], m_ref[:, here]], axis=0))
        held[k] = nn(left, jnp.concatenate([r_hi, r_hi], axis=0)) + nn(left, jnp.concatenate([r_lo, r_lo], axis=0))
        copies.append(pltpu.make_async_copy(held.at[k], out_ref.at[:, here], sems.at[k]))
        copies[k].start()
    for copy in copies:
        copy.wait()


def final(x, rows, chol, m, tile=1280):
    count, width = x.shape[1], chol.shape[1]
    return pl.pallas_call(
        final_kernel,
        out_shape=jax.ShapeDtypeStruct((count, width), F32),
        in_specs=[VMEM] * 4,
        out_specs=ANY,
        scratch_shapes=[pltpu.VMEM((width // tile, count, tile), F32), pltpu.SemaphoreType.DMA((width // tile,))],
        compiler_params=pltpu.CompilerParams(vmem_limit_bytes=30 * MIB),
        cost_estimate=pl.CostEstimate(flops=8 * count * 128 * width, bytes_accessed=10 * MIB, transcendentals=0),
    )(x, rows, chol, m)


def after(x, *others):
    return lax.optimization_barrier((x, *others))[0]


def body(slab_rows, slab_columns, chol, pairs):
    core = lax.axis_index("col") % 2
    zpart = lax.axis_index("row") // 4
    nchol, width = chol.shape

    picked = pick(pairs.reshape(16, 128), chol)
    u = prepare(slab_columns)
    own = jnp.sum(after(lax.all_to_all(picked, "col", 0, 0), u), axis=0)
    other = lax.ppermute(own, BOTH, ZPAIR)

    theirs = lax.ppermute(mirror(False, own, other, u), BOTH, CORE)
    part = (mirror(True, own, other, u) + theirs).reshape(8, 8, width)
    pieces = lax.all_to_all(part, "col", 0, 0, axis_index_groups=PLANE)

    x = contract(after(chol, part), slab_rows)
    for bit in (1, 2):
        x = x + lax.ppermute(x, BOTH, moves(lambda r, c: (r, c ^ bit)))
    panel = jnp.where(zpart == 0, jnp.concatenate([own, other]), jnp.concatenate([other, own]))
    panel = after(panel, part)
    partner = lax.ppermute(panel, BOTH, CORE)
    pair = jnp.stack([jnp.where(core == 0, panel, partner), jnp.where(core == 0, partner, panel)])
    rows = lax.ppermute(pair, BOTH, FLIP)

    turned = lax.ppermute(jnp.sum(after(pieces, x, rows), axis=0), BOTH, TURN)
    spread = jnp.broadcast_to(turned, (8,) + turned.shape)
    mirrored = lax.all_to_all(spread, "row", 0, 0).reshape(nchol, width)

    x = after(x, spread)
    for bit in (4, 8):
        x = x + lax.ppermute(x, BOTH, moves(lambda r, c: (r, c ^ bit)))
    return final(x, rows, chol, mirrored)


def solution(mesh):
    placed = (P("row", "col"), P("row", "col"), P(None, "col"), P())
    return jax.shard_map(
        body, mesh=mesh, in_specs=placed, out_specs=P("row", "col"), check_vma=False
    )
```

time: 143 us -> 118 us (0.83)
  the two profiles are of different devices: /device:TPU:0 before, /device:TPU:6 now
where the time goes in v2:
time: 118 us; the launch traced here: 117 us
  waiting for transfers between devices  56.3 us (48%)
  starting transfers between devices  32.3 us (27%)
  Pallas kernels  16.5 us (14%)
  local copies, waits for them, and re-layouts  9.77 us (8%)
  other arithmetic  2.33 us (2%)
    ppermute x4, waiting for transfers between devices, body(): x = x + lax.ppermute(x, BOTH, moves(lambda r, c: (r, c ^ bit)))  16.6 us
    ppermute x1, waiting for transfers between devices, body(): turned = lax.ppermute(jnp.sum(after(pieces, x, rows), axis=0), BOTH, TURN)  14.4 us
    all_to_all x1, waiting for transfers between devices, body(): mirrored = lax.all_to_all(spread, 'row', 0, 0).reshape(nchol, width)  12.2 us
    unnamed x8, local copies, waits for them, and re-layouts  8.5 us
    all_to_all x1, starting transfers between devices, body(): own = jnp.sum(after(lax.all_to_all(picked, 'col', 0, 0), u), axis=0)  8.13 us
    ppermute x1, waiting for transfers between devices, body(): rows = lax.ppermute(pair, BOTH, FLIP)  7.45 us
    all_to_all x1, starting transfers between devices, body(): pieces = lax.all_to_all(part, 'col', 0, 0, axis_index_groups=PLANE)  7.21 us
    ppermute x1, starting transfers between devices, body(): rows = lax.ppermute(pair, BOTH, FLIP)  5.53 us
  transfers between devices with their start and end apart: 12, of which 9 were waited for; matrix products, arithmetic and copies ran while one was open for 1% of the time, Pallas kernels for 7%

profile of v2, /device:TPU:6, one launch (start us, length us, event | category | flops | bytes accessed | tf_op | source)
XLA Modules:
  0.0 117.4 jit_solution(12924032038065455114)
XLA Ops:
  0.0 4.4 %shard_map.46 = f32[16,32,128]{2,1,0:T(8,128)} custom-call(s32[16,128]{1,0:T(8,128)} %bitcast.9, f32[64,6400]{1,0:T(8,128)} %chol_ref.4), custom_call_target="tpu_custom_call" | custom-call | tf_op jit(solution)/shard_map/pallas_call | solution.py:82
  4.5 8.1 %all-to-all-start = ((f32[16,32,128]{2,1,0:T(8,128)}), f32[16,32,128]{2,1,0:T(8,128)S(1)}, u32[]{:S(2)}, u32[]{:S(2)}) async-start(f32[16,32,128]{2,1,0:T(8,128)} %shard_map.46), calls=%async_computation | async-start | bytes 524288 | tf_op jit(solution)/shard_map/all_to_all | solution.py:210
  12.6 0.0 copy-start.3
  12.6 2.9 %copy-done.3 = f32[12800,128]{1,0:T(8,128)S(1)} copy-done((f32[12800,128]{1,0:T(8,128)S(1)}, f32[12800,128]{1,0:T(8,128)}, u32[]{:S(2)}) %copy-start.3) | copy-done | bytes 6553624
  15.4 2.4 %shard_map.47.refs_2_ = bf16[256,12800]{1,0:T(8,128)(2,1)S(1)} custom-call(f32[12800,128]{1,0:T(8,128)S(1)} %copy-done.3), custom_call_target="tpu_custom_call" | custom-call | bytes 13631488 | tf_op jit(solution)/shard_map/pallas_call | solution.py:100
  17.9 0.0 copy-start
  17.9 2.8 %copy-done = bf16[256,12800]{1,0:T(8,128)(2,1)} copy-done((bf16[256,12800]{1,0:T(8,128)(2,1)}, bf16[256,12800]{1,0:T(8,128)(2,1)S(1)}, u32[]{:S(2)}) %copy-start) | copy-done | bytes 6553624
  20.7 0.0 all-to-all-done
  20.7 1.1 collective-permute-start
  21.8 2.7 %collective-permute-done.refs_1_ = f32[32,128]{1,0:T(8,128)S(1)} collective-permute-done((f32[32,128]{1,0:T(8,128)S(1)}, f32[32,128]{1,0:T(8,128)S(1)}, u32[]{:S(2)}, u32[]{:S(2)}) %collective-permute-start) | collective-permute-done | bytes 16416 | tf_op jit(solution)/shard_map/ppermute | solution.py:211
  24.5 0.0 copy-start.1
  24.5 2.9 %copy-done.1 = bf16[256,12800]{1,0:T(8,128)(2,1)S(1)} copy-done((bf16[256,12800]{1,0:T(8,128)(2,1)S(1)}, bf16[256,12800]{1,0:T(8,128)(2,1)}, u32[]{:S(2)}) %copy-start.1) | copy-done | bytes 6553624
  27.4 0.6 shard_map.49
  28.0 0.1 collective-permute-start.1
  28.1 0.6 shard_map.48
  28.7 2.9 %collective-permute-done.1 = f32[64,6400]{1,0:T(8,128)S(1)} collective-permute-done((f32[64,6400]{1,0:T(8,128)S(1)}, f32[64,6400]{1,0:T(8,128)S(1)}, u32[]{:S(2)}, u32[]{:S(2)}) %collective-permute-start.1) | collective-permute-done | bytes 1638432 | tf_op jit(solution)/shard_map/ppermute | solution.py:213
  31.6 1.3 %add_bitcast_fusion = f32[8,8,6400]{2,1,0:T(8,128)} fusion(f32[64,6400]{1,0:T(8,128)S(1)} %shard_map.48, f32[64,6400]{1,0:T(8,128)S(1)} %collective-permute-done.1), kind=kLoop, calls=%fused_computation | loop fusion | flops 409600 | bytes 4915200 | tf_op jit(solution)/shard_map/reshape | solution.py:214
  32.9 7.2 %all-to-all-start.1 = ((f32[8,8,6400]{2,1,0:T(8,128)}), f32[8,8,6400]{2,1,0:T(8,128)S(1)}, u32[]{:S(2)}, u32[]{:S(2)}) async-start(f32[8,8,6400]{2,1,0:T(8,128)} %add_bitcast_fusion), calls=%async_computation.1 | async-start | bytes 3276800 | tf_op jit(solution)/shard_map/all_to_all | solution.py:215
  40.1 0.1 collective-permute-start.4
  40.2 5.1 %shard_map.50 = f32[64,256]{1,0:T(8,128)} custom-call(f32[64,6400]{1,0:T(8,128)} %chol_ref.4, f32[256,6400]{1,0:T(8,128)} %rows_ref.1), custom_call_target="tpu_custom_call" | custom-call | flops 629145600 | bytes 8192000 | tf_op jit(solution)/shard_map/pallas_call | solution.py:126
  45.3 0.5 collective-permute-start.2
  45.8 0.0 collective-permute-done.4
  45.8 1.1 collective-permute-done.2
  46.9 0.8 add.21
  47.8 3.0 %collective-permute-start.3 = (f32[64,256]{1,0:T(8,128)S(1)}, f32[64,256]{1,0:T(8,128)S(1)}, u32[]{:S(2)}, u32[]{:S(2)}) collective-permute-start(f32[64,256]{1,0:T(8,128)S(1)} %add.21), channel_id=1, source_target_pairs={{0,2},{1,3},{2,0},{3,1},{4,6},{5,7},{6,4},{7,5},{8,10},{9,11},{10,... | collective-permute-start | bytes 196616 | tf_op jit(solution)/shard_map/ppermute | solution.py:219
  50.8 5.5 %collective-permute-start.5 = (f32[2,64,128]{2,1,0:T(8,128)S(1)}, f32[2,64,128]{2,1,0:T(8,128)S(1)}, u32[]{:S(2)}, u32[]{:S(2)}) collective-permute-start(f32[2,64,128]{2,1,0:T(8,128)S(1)} %pad_maximum_fusion), channel_id=1, source_target_pairs={{0,0},{1,1},{2,16},{3,17},{4,32},{5,33},{6,48},{7,49},{8,64},{9,65... | collective-permute-start | bytes 196616 | tf_op jit(solution)/shard_map/ppermute | solution.py:224
  56.3 6.3 %collective-permute-done.3 = f32[64,256]{1,0:T(8,128)S(1)} collective-permute-done((f32[64,256]{1,0:T(8,128)S(1)}, f32[64,256]{1,0:T(8,128)S(1)}, u32[]{:S(2)}, u32[]{:S(2)}) %collective-permute-start.3) | collective-permute-done | bytes 65568 | tf_op jit(solution)/shard_map/ppermute | solution.py:219
  62.7 7.4 %collective-permute-done.5.rows_ref = f32[2,64,128]{2,1,0:T(8,128)S(1)} collective-permute-done((f32[2,64,128]{2,1,0:T(8,128)S(1)}, f32[2,64,128]{2,1,0:T(8,128)S(1)}, u32[]{:S(2)}, u32[]{:S(2)}) %collective-permute-start.5) | collective-permute-done | bytes 65568 | tf_op jit(solution)/shard_map/ppermute | solution.py:224
  70.1 0.0 all-to-all-done.1
  70.1 0.1 reduce_sum.19
  70.2 1.9 %collective-permute-start.6 = (f32[8,6400]{1,0:T(8,128)S(1)}, f32[8,6400]{1,0:T(8,128)S(1)}, u32[]{:S(2)}, u32[]{:S(2)}) collective-permute-start(f32[8,6400]{1,0:T(8,128)S(1)} %reduce_sum.19), channel_id=1, source_target_pairs={{0,32},{1,33},{2,64},{3,65},{4,16},{5,17},{6,80},{7,81},{8,0},{9,1... | collective-permute-start | bytes 614408 | tf_op jit(solution)/shard_map/ppermute | solution.py:226
  72.2 14.4 %collective-permute-done.6 = f32[8,6400]{1,0:T(8,128)S(1)} collective-permute-done((f32[8,6400]{1,0:T(8,128)S(1)}, f32[8,6400]{1,0:T(8,128)S(1)}, u32[]{:S(2)}, u32[]{:S(2)}) %collective-permute-start.6) | collective-permute-done | bytes 204832 | tf_op jit(solution)/shard_map/ppermute | solution.py:226
  86.6 1.3 %broadcast_in_dim.3 = f32[8,8,6400]{2,1,0:T(8,128)} broadcast(f32[8,6400]{1,0:T(8,128)S(1)} %collective-permute-done.6), dimensions={1,2} | broadcast | bytes 1843200 | tf_op jit(solution)/shard_map/broadcast_in_dim | solution.py:227
  87.8 0.0 copy-start.2
  87.8 3.7 %all-to-all-start.2 = ((f32[8,8,6400]{2,1,0:T(8,128)}), f32[8,8,6400]{2,1,0:T(8,128)S(1)}, u32[]{:S(2)}, u32[]{:S(2)}) async-start(f32[8,8,6400]{2,1,0:T(8,128)} %broadcast_in_dim.3), calls=%async_computation.2 | async-start | bytes 3276800 | tf_op jit(solution)/shard_map/all_to_all | solution.py:228
  91.6 0.9 collective-permute-start.7
  92.5 3.4 %collective-permute-done.7 = f32[64,256]{1,0:T(8,128)S(1)} collective-permute-done((f32[64,256]{1,0:T(8,128)S(1)}, f32[64,256]{1,0:T(8,128)S(1)}, u32[]{:S(2)}, u32[]{:S(2)}) %collective-permute-start.7) | collective-permute-done | bytes 65568 | tf_op jit(solution)/shard_map/ppermute | solution.py:232
  95.9 0.1 collective-permute-start.8
  96.0 5.8 %collective-permute-done.8 = f32[64,256]{1,0:T(8,128)S(1)} collective-permute-done((f32[64,256]{1,0:T(8,128)S(1)}, f32[64,256]{1,0:T(8,128)S(1)}, u32[]{:S(2)}, u32[]{:S(2)}) %collective-permute-start.8) | collective-permute-done | bytes 65568 | tf_op jit(solution)/shard_map/ppermute | solution.py:232
  101.8 12.2 %all-to-all-done.2 = f32[8,8,6400]{2,1,0:T(8,128)S(1)} async-done(((f32[8,8,6400]{2,1,0:T(8,128)}), f32[8,8,6400]{2,1,0:T(8,128)S(1)}, u32[]{:S(2)}, u32[]{:S(2)}) %all-to-all-start.2) | async-done | bytes 1638432 | tf_op jit(solution)/shard_map/all_to_all | solution.py:228
  114.0 0.0 copy-done.2
  114.0 3.4 %shard_map.51 = f32[256,6400]{1,0:T(8,128)} custom-call(f32[64,256]{1,0:T(8,128)S(1)} %add.25.x_ref, f32[2,64,128]{2,1,0:T(8,128)S(1)} %collective-permute-done.5.rows_ref, f32[64,6400]{1,0:T(8,128)S(1)} %copy-done.2, f32[64,6400]{1,0:T(8,128)S(1)} %bitcast.8), custom_call_target="tpu_custom_call" | custom-call | flops 1677721600 | bytes 10485760 | tf_op jit(solution)/shard_map/pallas_call | solution.py:188
  (7 shorter events, 0.1 us)
Async XLA Ops:
  4.5 16.2 %all-to-all-start = ((f32[16,32,128]{2,1,0:T(8,128)}), f32[16,32,128]{2,1,0:T(8,128)S(1)}, u32[]{:S(2)}, u32[]{:S(2)}) async-start(f32[16,32,128]{2,1,0:T(8,128)} %shard_map.46), calls=%async_computation | async-start | bytes 524288 | tf_op jit(solution)/shard_map/all_to_all | solution.py:210
  12.6 2.9 %copy-start.3 = (f32[12800,128]{1,0:T(8,128)S(1)}, f32[12800,128]{1,0:T(8,128)}, u32[]{:S(2)}) copy-start(f32[12800,128]{1,0:T(8,128)} %u_ref.1) | copy-start | bytes 19660804
  17.9 2.8 %copy-start = (bf16[256,12800]{1,0:T(8,128)(2,1)}, bf16[256,12800]{1,0:T(8,128)(2,1)S(1)}, u32[]{:S(2)}) copy-start(bf16[256,12800]{1,0:T(8,128)(2,1)S(1)} %shard_map.47.refs_2_) | copy-start | bytes 19660804
  20.7 3.8 %collective-permute-start = (f32[32,128]{1,0:T(8,128)S(1)}, f32[32,128]{1,0:T(8,128)S(1)}, u32[]{:S(2)}, u32[]{:S(2)}) collective-permute-start(f32[32,128]{1,0:T(8,128)S(1)} %reduce_sum.18.refs_0_), channel_id=1, source_target_pairs={{0,64},{1,65},{2,66},{3,67},{4,68},{5,69},{6,70},{7,71},{8,72},{9,... | collective-permute-start | bytes 49160 | tf_op jit(solution)/shard_map/ppermute | solution.py:211
  24.5 2.9 %copy-start.1 = (bf16[256,12800]{1,0:T(8,128)(2,1)S(1)}, bf16[256,12800]{1,0:T(8,128)(2,1)}, u32[]{:S(2)}) copy-start(bf16[256,12800]{1,0:T(8,128)(2,1)} %copy-done) | copy-start | bytes 19660804
  28.0 3.6 %collective-permute-start.1 = (f32[64,6400]{1,0:T(8,128)S(1)}, f32[64,6400]{1,0:T(8,128)S(1)}, u32[]{:S(2)}, u32[]{:S(2)}) collective-permute-start(f32[64,6400]{1,0:T(8,128)S(1)} %shard_map.49), channel_id=1, source_target_pairs={{0,1},{1,0},{2,3},{3,2},{4,5},{5,4},{6,7},{7,6},{8,9},{9,8},{10,11... | collective-permute-start | bytes 4915208 | tf_op jit(solution)/shard_map/ppermute | solution.py:213
  32.9 37.2 %all-to-all-start.1 = ((f32[8,8,6400]{2,1,0:T(8,128)}), f32[8,8,6400]{2,1,0:T(8,128)S(1)}, u32[]{:S(2)}, u32[]{:S(2)}) async-start(f32[8,8,6400]{2,1,0:T(8,128)} %add_bitcast_fusion), calls=%async_computation.1 | async-start | bytes 3276800 | tf_op jit(solution)/shard_map/all_to_all | solution.py:215
  40.1 5.7 %collective-permute-start.4 = (f32[64,128]{1,0:T(8,128)S(1)}, f32[64,128]{1,0:T(8,128)S(1)}, u32[]{:S(2)}, u32[]{:S(2)}) collective-permute-start(f32[64,128]{1,0:T(8,128)S(1)} %maximum_select_fusion), channel_id=1, source_target_pairs={{0,1},{1,0},{2,3},{3,2},{4,5},{5,4},{6,7},{7,6},{8,9},{9,8},{10,11... | collective-permute-start | bytes 98312 | tf_op jit(solution)/shard_map/ppermute | solution.py:222
  45.3 1.6 %collective-permute-start.2 = (f32[64,256]{1,0:T(8,128)}, f32[64,256]{1,0:T(8,128)S(1)}, u32[]{:S(2)}, u32[]{:S(2)}) collective-permute-start(f32[64,256]{1,0:T(8,128)} %shard_map.50), channel_id=1, source_target_pairs={{0,1},{1,0},{2,3},{3,2},{4,5},{5,4},{6,7},{7,6},{8,9},{9,8},{10,11... | collective-permute-start | bytes 196616 | tf_op jit(solution)/shard_map/ppermute | solution.py:219
  47.8 14.9 %collective-permute-start.3 = (f32[64,256]{1,0:T(8,128)S(1)}, f32[64,256]{1,0:T(8,128)S(1)}, u32[]{:S(2)}, u32[]{:S(2)}) collective-permute-start(f32[64,256]{1,0:T(8,128)S(1)} %add.21), channel_id=1, source_target_pairs={{0,2},{1,3},{2,0},{3,1},{4,6},{5,7},{6,4},{7,5},{8,10},{9,11},{10,... | collective-permute-start | bytes 196616 | tf_op jit(solution)/shard_map/ppermute | solution.py:219
  50.8 19.3 %collective-permute-start.5 = (f32[2,64,128]{2,1,0:T(8,128)S(1)}, f32[2,64,128]{2,1,0:T(8,128)S(1)}, u32[]{:S(2)}, u32[]{:S(2)}) collective-permute-start(f32[2,64,128]{2,1,0:T(8,128)S(1)} %pad_maximum_fusion), channel_id=1, source_target_pairs={{0,0},{1,1},{2,16},{3,17},{4,32},{5,33},{6,48},{7,49},{8,64},{9,65... | collective-permute-start | bytes 196616 | tf_op jit(solution)/shard_map/ppermute | solution.py:224
  70.2 16.3 %collective-permute-start.6 = (f32[8,6400]{1,0:T(8,128)S(1)}, f32[8,6400]{1,0:T(8,128)S(1)}, u32[]{:S(2)}, u32[]{:S(2)}) collective-permute-start(f32[8,6400]{1,0:T(8,128)S(1)} %reduce_sum.19), channel_id=1, source_target_pairs={{0,32},{1,33},{2,64},{3,65},{4,16},{5,17},{6,80},{7,81},{8,0},{9,1... | collective-permute-start | bytes 614408 | tf_op jit(solution)/shard_map/ppermute | solution.py:226
  87.8 26.1 %copy-start.2 = (f32[64,6400]{1,0:T(8,128)S(1)}, f32[64,6400]{1,0:T(8,128)}, u32[]{:S(2)}) copy-start(f32[64,6400]{1,0:T(8,128)} %chol_ref.4) | copy-start | bytes 4915204
  87.8 26.1 %all-to-all-start.2 = ((f32[8,8,6400]{2,1,0:T(8,128)}), f32[8,8,6400]{2,1,0:T(8,128)S(1)}, u32[]{:S(2)}, u32[]{:S(2)}) async-start(f32[8,8,6400]{2,1,0:T(8,128)} %broadcast_in_dim.3), calls=%async_computation.2 | async-start | bytes 3276800 | tf_op jit(solution)/shard_map/all_to_all | solution.py:228
  91.6 4.3 %collective-permute-start.7 = (f32[64,256]{1,0:T(8,128)S(1)}, f32[64,256]{1,0:T(8,128)S(1)}, u32[]{:S(2)}, u32[]{:S(2)}) collective-permute-start(f32[64,256]{1,0:T(8,128)S(1)} %add.22), channel_id=1, source_target_pairs={{0,4},{1,5},{2,6},{3,7},{4,0},{5,1},{6,2},{7,3},{8,12},{9,13},{10,... | collective-permute-start | bytes 196616 | tf_op jit(solution)/shard_map/ppermute | solution.py:232
  95.9 5.8 %collective-permute-start.8 = (f32[64,256]{1,0:T(8,128)S(1)}, f32[64,256]{1,0:T(8,128)S(1)}, u32[]{:S(2)}, u32[]{:S(2)}) collective-permute-start(f32[64,256]{1,0:T(8,128)S(1)} %add.24), channel_id=1, source_target_pairs={{0,8},{1,9},{2,10},{3,11},{4,12},{5,13},{6,14},{7,15},{8,0},{9,1},... | collective-permute-start | bytes 196616 | tf_op jit(solution)/shard_map/ppermute | solution.py:232

commit v3 on v2

v3 whole, which is shorter than its diff:
```python
import jax
import jax.numpy as jnp
import numpy as np
from jax import lax
from jax.experimental import pallas as pl
from jax.experimental.pallas import tpu as pltpu
from jax.sharding import PartitionSpec as P

F32, BF16 = jnp.float32, jnp.bfloat16
MIB = 1024 * 1024
BOTH = ("row", "col")

SLOT = np.array(
    [
        [2, 6, 1, 4, 7, 0, 3, 5],
        [0, 7, 4, 2, 6, 1, 5, 3],
        [0, 7, 3, 4, 1, 5, 2, 6],
        [7, 1, 5, 2, 4, 0, 6, 3],
        [7, 3, 4, 1, 6, 0, 2, 5],
        [3, 7, 0, 4, 1, 6, 5, 2],
        [6, 2, 5, 1, 0, 3, 4, 7],
        [1, 6, 2, 0, 3, 5, 7, 4],
    ],
    np.int32,
)
CODE = [sum(int(v) << (3 * j) for j, v in enumerate(line)) for line in SLOT]
PLANE = [[2 * j + k for j in range(8)] for k in range(2)]


def moves(to):
    return [(r * 16 + c, (lambda d: d[0] * 16 + d[1])(to(r, c))) for r in range(8) for c in range(16)]


CORE = moves(lambda r, c: (r, c ^ 1))
ZPAIR = moves(lambda r, c: (r ^ 4, c))
TURN = moves(lambda r, c: (int(SLOT[r, c // 2]), 2 * r + c % 2))

VMEM = pl.BlockSpec(memory_space=pltpu.VMEM)
ANY = pl.BlockSpec(memory_space=pl.ANY)


def split(x):
    hi = x.astype(BF16)
    return hi, (x - hi.astype(F32)).astype(BF16)


def nt(a, b):
    return lax.dot_general(a, b, (((1,), (1,)), ((), ())), preferred_element_type=F32)


def nn(a, b):
    return lax.dot_general(a, b, (((1,), (0,)), ((), ())), preferred_element_type=F32)


def panel_kernel(pairs_ref, chol_ref, rows_ref, keep_ref, send_ref, chol_held, rows_held, sems):
    nchol, width = chol_held.shape
    half = nchol // 2
    tiles = width // 128
    steps = rows_held.shape[0]
    chunk = width // steps
    load_chol = pltpu.make_async_copy(chol_ref, chol_held, sems.at[steps])
    load_chol.start()
    loads = []
    for k in range(steps):
        here = pl.ds(k * chunk, chunk)
        loads.append(pltpu.make_async_copy(rows_ref.at[:, here], rows_held.at[k], sems.at[k]))
        loads[k].start()
    row = lax.axis_index("row")
    col = lax.axis_index("col")
    first = lax.rem(col, 2) == 0
    lanes = lax.broadcasted_iota(jnp.int32, (128, 128), 0)

    def put(j, where, pair):
        keep_ref[j, where, :] = jnp.where(first, pair[:, :128], pair[:, 128:])
        send_ref[j, where, :] = jnp.where(first, pair[:, 128:], pair[:, :128])

    load_chol.wait()
    mine = chol_held.at[pl.ds(pl.multiple_of(row // 4 * half, half), half), :]
    stack = jnp.concatenate([mine[:, t * 128 : t * 128 + 128] for t in range(tiles)], axis=0)
    stack = jnp.concatenate(split(stack), axis=1)
    for j in range(8):
        index = [pairs_ref[2 * j + i : 2 * j + i + 1, :] - col * width for i in range(2)]
        hot = jnp.concatenate([jnp.where(lanes == (i & 127), 1.0, 0.0) for i in index], axis=1).astype(BF16)
        found = nn(stack, jnp.concatenate([hot, hot], axis=0))
        tile = jnp.broadcast_to(jnp.concatenate([i >> 7 for i in index], axis=1), (half, 256))
        total = jnp.zeros((half, 256), F32)
        for t in range(tiles):
            total = jnp.where(tile == t, found[t * half : t * half + half], total)
        put(j, slice(0, half), total)
    for ref in (keep_ref, send_ref):
        for j in range(8):
            there = row if j < 4 else row ^ 4
            ref[j, half : half + 8, :] = ref[there, 8 * (j % 4) : 8 * (j % 4) + 8, :]
    total = jnp.zeros((rows_held.shape[1], 2 * nchol), F32)
    for k in range(steps):
        loads[k].wait()
        a = jnp.concatenate(split(chol_held[:, k * chunk : k * chunk + chunk]), axis=0)
        b_hi, b_lo = split(rows_held[k])
        total += nt(b_hi, a) + nt(b_lo, a)
    total = total.T
    x = total[:nchol] + total[nchol:]
    for j in range(8):
        put(j, slice(half + 8, half + 16), x[8 * j : 8 * j + 8])


def panel_pieces(pairs, chol, rows, steps=2):
    nchol, width = chol.shape
    return pl.pallas_call(
        panel_kernel,
        out_shape=[jax.ShapeDtypeStruct((8, nchol // 2 + 16, 128), F32)] * 2,
        in_specs=[VMEM, ANY, ANY],
        out_specs=[VMEM, VMEM],
        scratch_shapes=[
            pltpu.VMEM(chol.shape, F32),
            pltpu.VMEM((steps, rows.shape[0], width // steps), F32),
            pltpu.SemaphoreType.DMA((steps + 1,)),
        ],
        compiler_params=pltpu.CompilerParams(vmem_limit_bytes=57 * MIB),
    )(pairs, chol, rows)


def prepare_kernel(u_ref, out_ref):
    width = out_ref.shape[1]
    start = pl.multiple_of((1 - lax.rem(lax.axis_index("col"), 2)) * width, width)
    hi, lo = split(u_ref[pl.ds(start, width), :].T)
    out_ref[:128, :] = hi
    out_ref[128:, :] = lo


def prepare(u):
    count, span = u.shape
    return pl.pallas_call(
        prepare_kernel,
        out_shape=jax.ShapeDtypeStruct((2 * span, count // 2), BF16),
        in_specs=[VMEM],
        out_specs=VMEM,
        compiler_params=pltpu.CompilerParams(vmem_limit_bytes=30 * MIB),
        cost_estimate=pl.CostEstimate(flops=0, bytes_accessed=7 * MIB, transcendentals=0),
    )(u)


def mirror_kernel(own_ref, other_ref, u_ref, out_ref):
    width = out_ref.shape[1]
    if u_ref.dtype == BF16:
        u = u_ref[...]
    else:
        start = pl.multiple_of(lax.rem(lax.axis_index("col"), 2) * width, width)
        u = jnp.concatenate(split(u_ref[pl.ds(start, width), :].T), axis=0)
    row = lax.axis_index("row")
    code = jnp.int32(CODE[0])
    for r in range(1, 8):
        code = jnp.where(row == r, jnp.int32(CODE[r]), code)
    slices = []
    for j in range(8):
        at = (code >> (3 * j)) & 7
        rows = pl.ds(pl.multiple_of((at & 3) * 8, 8), 8)
        slices.append(jnp.where((at >> 2) == (row >> 2), own_ref[rows, :], other_ref[rows, :]))
    hi, lo = split(jnp.concatenate(slices, axis=0))
    top = jnp.concatenate([hi, hi], axis=1)
    low = jnp.concatenate([lo, jnp.zeros_like(lo)], axis=1)
    both = nn(jnp.concatenate([top, low], axis=0), u)
    out_ref[...] = both[:64] + both[64:]


def mirror(own, other, u, width):
    return pl.pallas_call(
        mirror_kernel,
        out_shape=jax.ShapeDtypeStruct((64, width), F32),
        in_specs=[VMEM] * 3,
        out_specs=VMEM,
        compiler_params=pltpu.CompilerParams(vmem_limit_bytes=30 * MIB),
        cost_estimate=pl.CostEstimate(flops=6 * 64 * 128 * width, bytes_accessed=5 * MIB, transcendentals=0),
    )(own, other, u)


def join_kernel(mine_ref, theirs_ref, own_ref, other_ref, partner_ref, out_ref):
    width = mine_ref.shape[1]
    half = own_ref.shape[0] - 16
    col = lax.axis_index("col")
    out_ref[:, :, :width] = (mine_ref[...] + theirs_ref[...]).reshape(8, 8, width)
    first = lax.rem(col, 2) == 0
    mine, partner = own_ref[half + 8 :, :], partner_ref[half + 8 :, :]
    rows = slice(half, half + 8)
    panel = jnp.where(col < 8, own_ref[rows, :], other_ref[rows, :])
    extra = jnp.concatenate([jnp.where(first, mine, partner), jnp.where(first, partner, mine), panel], axis=1)
    for j in range(8):
        out_ref[j, :, width:] = extra


def join(mine, theirs, own, other, partner):
    return pl.pallas_call(
        join_kernel,
        out_shape=jax.ShapeDtypeStruct((8, 8, mine.shape[1] + 384), F32),
        in_specs=[VMEM] * 5,
        out_specs=VMEM,
        compiler_params=pltpu.CompilerParams(vmem_limit_bytes=30 * MIB),
    )(mine, theirs, own, other, partner)


def final_kernel(x_ref, mine_ref, partner_ref, chol_ref, m_ref, out_ref, held, sems):
    tile = held.shape[2]
    half = mine_ref.shape[0] // 2
    first = lax.rem(lax.axis_index("col"), 2) == 0
    rows = [jnp.where(first, mine_ref[...], partner_ref[...]), jnp.where(first, partner_ref[...], mine_ref[...])]
    rows = jnp.concatenate(rows, axis=1)
    low = lax.axis_index("row") < 4
    rows = [jnp.where(low, rows[:half], rows[half:]), jnp.where(low, rows[half:], rows[:half])]
    left = jnp.concatenate([x_ref[...], *rows], axis=0).T
    left = jnp.concatenate(split(left), axis=1)
    copies = []
    for k in range(held.shape[0]):
        here = slice(k * tile, k * tile + tile)
        r_hi, r_lo = split(jnp.concatenate([chol_ref[:, here], m_ref[:, here]], axis=0))
        held[k] = nn(left, jnp.concatenate([r_hi, r_hi], axis=0)) + nn(left, jnp.concatenate([r_lo, r_lo], axis=0))
        copies.append(pltpu.make_async_copy(held.at[k], out_ref.at[:, here], sems.at[k]))
        copies[k].start()
    for copy in copies:
        copy.wait()


def final(x, mine, partner, chol, m, tile=1280):
    count, width = x.shape[1], chol.shape[1]
    return pl.pallas_call(
        final_kernel,
        out_shape=jax.ShapeDtypeStruct((count, width), F32),
        in_specs=[VMEM] * 5,
        out_specs=ANY,
        scratch_shapes=[pltpu.VMEM((width // tile, count, tile), F32), pltpu.SemaphoreType.DMA((width // tile,))],
        compiler_params=pltpu.CompilerParams(vmem_limit_bytes=30 * MIB),
        cost_estimate=pl.CostEstimate(flops=8 * count * 128 * width, bytes_accessed=10 * MIB, transcendentals=0),
    )(x, mine, partner, chol, m)


def after(x, *others):
    return lax.optimization_barrier((x, *others))[0]


def body(slab_rows, slab_columns, chol, pairs):
    nchol, width = chol.shape

    keep, send = panel_pieces(pairs.reshape(16, 128), chol, slab_rows)
    pieces = keep + lax.ppermute(send, BOTH, CORE)
    own = jnp.sum(lax.all_to_all(pieces, "col", 0, 0, axis_index_groups=PLANE), axis=0)
    other = lax.ppermute(own, BOTH, ZPAIR)
    partner = lax.ppermute(own, BOTH, CORE)

    theirs = mirror(own, other, prepare(after(slab_columns, own)), slab_columns.shape[0] // 2)
    theirs = lax.ppermute(theirs, BOTH, CORE)
    mine = mirror(own, other, slab_columns, slab_columns.shape[0] // 2)
    part = join(mine, theirs, own, other, partner)
    got = lax.all_to_all(part, "col", 0, 0, axis_index_groups=PLANE)
    x = got[:, :, width : width + 256].reshape(nchol, 256)
    rows = got[:, :, width + 256 :].reshape(nchol, 128)

    turned = lax.ppermute(jnp.sum(got[:, :, :width], axis=0), BOTH, TURN)
    partner = lax.ppermute(rows, BOTH, CORE)
    spread = after(jnp.broadcast_to(turned, (8,) + turned.shape), x, rows, partner)
    mirrored = lax.all_to_all(spread, "row", 0, 0).reshape(nchol, width)
    return final(x, rows, partner, chol, mirrored)


def solution(mesh):
    placed = (P("row", "col"), P("row", "col"), P(None, "col"), P())
    return jax.shard_map(
        body, mesh=mesh, in_specs=placed, out_specs=P("row", "col"), check_vma=False
    )
```

time: 118 us -> 109 us (0.924)
  the two profiles are of different devices: /device:TPU:6 before, /device:TPU:0 now
where the time goes in v3:
time: 109 us
  blocking collectives  72.6 us (67%)
  Pallas kernels  13.2 us (12%)
  waiting for transfers between devices  13.2 us (12%)
  starting transfers between devices  5.03 us (5%)
  local copies, waits for them, and re-layouts  3.72 us (3%)
    all_to_all x1, blocking collectives, body(): mirrored = lax.all_to_all(spread, 'row', 0, 0).reshape(nchol, width)  28.9 us
    all_to_all x1, blocking collectives, body(): got = lax.all_to_all(part, 'col', 0, 0, axis_index_groups=PLANE)  27.8 us
    all_to_all x1, blocking collectives, body(): lax.all_to_all(pieces, 'col', 0, 0, axis_index_groups=PLANE)  15.9 us
    ppermute x1, waiting for transfers between devices, body(): turned = lax.ppermute(jnp.sum(got[:, :, :width], axis=0), BOTH, TURN)  10.4 us
    pallas_call x1, Pallas kernels, panel_pieces(): pl.pallas_call(panel_kernel, out_shape=[jax.ShapeDtypeStruct((8, nchol //...  6.96 us
    unnamed x6, local copies, waits for them, and re-layouts  3.6 us
    pallas_call x1, Pallas kernels, final(): pl.pallas_call(final_kernel, out_shape=jax.ShapeDtypeStruct((count, width...  3.37 us
    ppermute x1, starting transfers between devices, body(): turned = lax.ppermute(jnp.sum(got[:, :, :width], axis=0), BOTH, TURN)  3.26 us
  transfers between devices with their start and end apart: 6, of which 3 were waited for; matrix products, arithmetic and copies ran while one was open for 0% of the time, Pallas kernels for 2%

profile of v3, /device:TPU:0, one launch (start us, length us, event | category | flops | bytes accessed | tf_op | source)
XLA Modules:
  0.0 108.9 jit_solution(8290784067479853185)
XLA Ops:
  0.0 7.0 %shard_map.46 = (f32[8,48,128]{2,1,0:T(8,128)}, f32[8,48,128]{2,1,0:T(8,128)}) custom-call(s32[16,128]{1,0:T(8,128)} %bitcast.7, f32[64,6400]{1,0:T(8,128)} %chol_ref.3, f32[256,6400]{1,0:T(8,128)} %rows_ref.1), custom_call_target="tpu_custom_call" | custom-call | tf_op jit(solution)/shard_map/pallas_call | solution.py:108
  7.0 0.1 collective-permute-start
  7.1 1.6 %collective-permute-done = f32[8,48,128]{2,1,0:T(8,128)S(1)} collective-permute-done((f32[8,48,128]{2,1,0:T(8,128)}, f32[8,48,128]{2,1,0:T(8,128)S(1)}, u32[]{:S(2)}, u32[]{:S(2)}) %collective-permute-start) | collective-permute-done | bytes 196640 | tf_op jit(solution)/shard_map/ppermute | solution.py:242
  8.7 1.0 add.3
  9.7 15.9 %all_to_all.15 = f32[8,48,128]{2,1,0:T(8,128)S(1)} all-to-all(f32[8,48,128]{2,1,0:T(8,128)S(1)} %add.3), channel_id=1, replica_groups={{0,2,4,6,8,10,12,14},{1,3,5,7,9,11,13,15},{16,18,20,22,24,26,28,30},{17..., dimensions={0} | all-to-all | bytes 393216 | tf_op jit(solution)/shard_map/all_to_all | solution.py:243
  25.6 1.1 %collective-permute-start.1 = (f32[48,128]{1,0:T(8,128)S(1)}, f32[48,128]{1,0:T(8,128)S(1)}, u32[]{:S(2)}, u32[]{:S(2)}) collective-permute-start(f32[48,128]{1,0:T(8,128)S(1)} %reduce_sum.18.own_ref), channel_id=1, source_target_pairs={{0,64},{1,65},{2,66},{3,67},{4,68},{5,69},{6,70},{7,71},{8,72},{9,... | collective-permute-start | bytes 73736 | tf_op jit(solution)/shard_map/ppermute | solution.py:244
  26.7 0.0 copy-start
  26.7 2.9 %copy-done = f32[12800,128]{1,0:T(8,128)S(1)} copy-done((f32[12800,128]{1,0:T(8,128)S(1)}, f32[12800,128]{1,0:T(8,128)}, u32[]{:S(2)}) %copy-start) | copy-done | bytes 6553624
  29.5 0.0 copy-start.1
  29.5 0.9 shard_map.48.u_ref
  30.5 0.0 collective-permute-done.1.other_ref
  30.5 0.6 shard_map.49
  31.1 0.1 collective-permute-start.2
  31.2 0.5 collective-permute-start.3
  31.7 0.7 copy-done.1
  32.4 1.1 %shard_map.47.mine_ref = f32[64,6400]{1,0:T(8,128)S(1)} custom-call(f32[48,128]{1,0:T(8,128)S(1)} %reduce_sum.18.own_ref, f32[48,128]{1,0:T(8,128)S(1)} %collective-permute-done.1.other_ref, f32[12800,128]{1,0:T(8,128)S(1)} %copy-done.1), custom_call_target="tpu_custom_call" | custom-call | flops 314572800 | bytes 5242880 | tf_op jit(solution)/shard_map/pallas_call | solution.py:166
  33.5 1.2 %collective-permute-done.3.partner_ref = f32[48,128]{1,0:T(8,128)S(1)} collective-permute-done((f32[48,128]{1,0:T(8,128)S(1)}, f32[48,128]{1,0:T(8,128)S(1)}, u32[]{:S(2)}, u32[]{:S(2)}) %collective-permute-start.3) | collective-permute-done | bytes 24608 | tf_op jit(solution)/shard_map/ppermute | solution.py:245
  34.7 0.0 collective-permute-done.2.theirs_ref
  34.7 0.2 shard_map.50
  34.9 27.8 %all_to_all.16 = f32[8,8,6784]{2,1,0:T(8,128)S(1)} all-to-all(f32[8,8,6784]{2,1,0:T(8,128)S(1)} %shard_map.50), channel_id=1, replica_groups={{0,2,4,6,8,10,12,14},{1,3,5,7,9,11,13,15},{16,18,20,22,24,26,28,30},{17..., dimensions={0} | all-to-all | bytes 3473408 | tf_op jit(solution)/shard_map/all_to_all | solution.py:251
  62.8 0.0 collective-permute-start.4
  62.8 0.1 slice_reduce_fusion
  62.8 3.3 %collective-permute-start.5 = (f32[8,6400]{1,0:T(8,128)S(1)}, f32[8,6400]{1,0:T(8,128)S(1)}, u32[]{:S(2)}, u32[]{:S(2)}) collective-permute-start(f32[8,6400]{1,0:T(8,128)S(1)} %slice_reduce_fusion), channel_id=1, source_target_pairs={{0,32},{1,33},{2,96},{3,97},{4,16},{5,17},{6,64},{7,65},{8,112},{9... | collective-permute-start | bytes 614408 | tf_op jit(solution)/shard_map/ppermute | solution.py:255
  66.1 0.0 collective-permute-done.4.partner_ref
  66.1 10.4 %collective-permute-done.5 = f32[8,6400]{1,0:T(8,128)S(1)} collective-permute-done((f32[8,6400]{1,0:T(8,128)S(1)}, f32[8,6400]{1,0:T(8,128)S(1)}, u32[]{:S(2)}, u32[]{:S(2)}) %collective-permute-start.5) | collective-permute-done | bytes 204832 | tf_op jit(solution)/shard_map/ppermute | solution.py:255
  76.6 0.1 broadcast_in_dim.3
  76.7 0.0 copy-start.2
  76.7 28.9 %all_to_all.17 = f32[8,8,6400]{2,1,0:T(8,128)S(1)} all-to-all(f32[8,8,6400]{2,1,0:T(8,128)S(1)} %broadcast_in_dim.3), channel_id=1, replica_groups=mesh['row'=8,'col'=16] {'row'}, dimensions={0} | all-to-all | bytes 3276800 | tf_op jit(solution)/shard_map/all_to_all | solution.py:258
  105.5 0.0 copy-done.2
  105.5 3.4 %shard_map.51 = f32[256,6400]{1,0:T(8,128)} custom-call(f32[64,256]{1,0:T(8,128)S(1)} %slice_bitcast_fusion.x_ref, f32[64,128]{1,0:T(8,128)S(1)} %slice_bitcast_fusion.1.mine_ref, f32[64,128]{1,0:T(8,128)S(1)} %collective-permute-done.4.partner_ref, f32[64,6400]{1,0:T(8,128)S(1)} %copy-done.2, f32[64,6400]{1,0:T(8,128)S(1)} %bitcast.6), custom_call_target="tpu_custom_call" | custom-call | flops 1677721600 | bytes 10485760 | tf_op jit(solution)/shard_map/pallas_call | solution.py:223
  (3 shorter events, 0.0 us)
Async XLA Ops:
  7.0 1.7 %collective-permute-start = (f32[8,48,128]{2,1,0:T(8,128)}, f32[8,48,128]{2,1,0:T(8,128)S(1)}, u32[]{:S(2)}, u32[]{:S(2)}) collective-permute-start(f32[8,48,128]{2,1,0:T(8,128)} %get-tuple-element.10), channel_id=1, source_target_pairs={{0,1},{1,0},{2,3},{3,2},{4,5},{5,4},{6,7},{7,6},{8,9},{9,8},{10,11... | collective-permute-start | bytes 589832 | tf_op jit(solution)/shard_map/ppermute | solution.py:242
  25.6 4.9 %collective-permute-start.1 = (f32[48,128]{1,0:T(8,128)S(1)}, f32[48,128]{1,0:T(8,128)S(1)}, u32[]{:S(2)}, u32[]{:S(2)}) collective-permute-start(f32[48,128]{1,0:T(8,128)S(1)} %reduce_sum.18.own_ref), channel_id=1, source_target_pairs={{0,64},{1,65},{2,66},{3,67},{4,68},{5,69},{6,70},{7,71},{8,72},{9,... | collective-permute-start | bytes 73736 | tf_op jit(solution)/shard_map/ppermute | solution.py:244
  26.7 2.9 %copy-start = (f32[12800,128]{1,0:T(8,128)S(1)}, f32[12800,128]{1,0:T(8,128)}, u32[]{:S(2)}) copy-start(f32[12800,128]{1,0:T(8,128)} %u_ref.2) | copy-start | bytes 19660804
  29.5 2.9 %copy-start.1 = (f32[12800,128]{1,0:T(8,128)S(1)}, f32[12800,128]{1,0:T(8,128)}, u32[]{:S(2)}) copy-start(f32[12800,128]{1,0:T(8,128)} %u_ref.2) | copy-start | bytes 19660804
  31.1 3.6 %collective-permute-start.2 = (f32[64,6400]{1,0:T(8,128)S(1)}, f32[64,6400]{1,0:T(8,128)S(1)}, u32[]{:S(2)}, u32[]{:S(2)}) collective-permute-start(f32[64,6400]{1,0:T(8,128)S(1)} %shard_map.49), channel_id=1, source_target_pairs={{0,1},{1,0},{2,3},{3,2},{4,5},{5,4},{6,7},{7,6},{8,9},{9,8},{10,11... | collective-permute-start | bytes 4915208 | tf_op jit(solution)/shard_map/ppermute | solution.py:248
  31.2 3.5 %collective-permute-start.3 = (f32[48,128]{1,0:T(8,128)S(1)}, f32[48,128]{1,0:T(8,128)S(1)}, u32[]{:S(2)}, u32[]{:S(2)}) collective-permute-start(f32[48,128]{1,0:T(8,128)S(1)} %reduce_sum.18.own_ref), channel_id=1, source_target_pairs={{0,1},{1,0},{2,3},{3,2},{4,5},{5,4},{6,7},{7,6},{8,9},{9,8},{10,11... | collective-permute-start | bytes 73736 | tf_op jit(solution)/shard_map/ppermute | solution.py:245
  62.8 3.4 %collective-permute-start.4 = (f32[64,128]{1,0:T(8,128)S(1)}, f32[64,128]{1,0:T(8,128)S(1)}, u32[]{:S(2)}, u32[]{:S(2)}) collective-permute-start(f32[64,128]{1,0:T(8,128)S(1)} %slice_bitcast_fusion.1.mine_ref), channel_id=1, source_target_pairs={{0,1},{1,0},{2,3},{3,2},{4,5},{5,4},{6,7},{7,6},{8,9},{9,8},{10,11... | collective-permute-start | bytes 98312 | tf_op jit(solution)/shard_map/ppermute | solution.py:256
  62.8 13.7 %collective-permute-start.5 = (f32[8,6400]{1,0:T(8,128)S(1)}, f32[8,6400]{1,0:T(8,128)S(1)}, u32[]{:S(2)}, u32[]{:S(2)}) collective-permute-start(f32[8,6400]{1,0:T(8,128)S(1)} %slice_reduce_fusion), channel_id=1, source_target_pairs={{0,32},{1,33},{2,96},{3,97},{4,16},{5,17},{6,64},{7,65},{8,112},{9... | collective-permute-start | bytes 614408 | tf_op jit(solution)/shard_map/ppermute | solution.py:255
  76.7 28.9 %copy-start.2 = (f32[64,6400]{1,0:T(8,128)S(1)}, f32[64,6400]{1,0:T(8,128)}, u32[]{:S(2)}) copy-start(f32[64,6400]{1,0:T(8,128)} %chol_ref.3) | copy-start | bytes 4915204

commit v4 on v3

--- a/solution.py
+++ b/solution.py
@@ -12,14 +12,14 @@
 
 SLOT = np.array(
     [
-        [2, 6, 1, 4, 7, 0, 3, 5],
-        [0, 7, 4, 2, 6, 1, 5, 3],
-        [0, 7, 3, 4, 1, 5, 2, 6],
-        [7, 1, 5, 2, 4, 0, 6, 3],
-        [7, 3, 4, 1, 6, 0, 2, 5],
-        [3, 7, 0, 4, 1, 6, 5, 2],
-        [6, 2, 5, 1, 0, 3, 4, 7],
-        [1, 6, 2, 0, 3, 5, 7, 4],
+        [2, 4, 0, 5, 1, 6, 3, 7],
+        [7, 0, 6, 3, 5, 2, 4, 1],
+        [3, 7, 0, 2, 1, 6, 5, 4],
+        [7, 1, 2, 0, 6, 3, 4, 5],
+        [4, 3, 6, 1, 7, 0, 2, 5],
+        [5, 2, 0, 4, 3, 7, 1, 6],
+        [4, 2, 7, 0, 6, 1, 5, 3],
+        [7, 4, 1, 2, 3, 5, 0, 6],
     ],
     np.int32,
 )
@@ -121,8 +121,7 @@
 
 def prepare_kernel(u_ref, out_ref):
     width = out_ref.shape[1]
-    start = pl.multiple_of((1 - lax.rem(lax.axis_index("col"), 2)) * width, width)
-    hi, lo = split(u_ref[pl.ds(start, width), :].T)
+    hi, lo = split(u_ref[...].T)
     out_ref[:128, :] = hi
     out_ref[128:, :] = lo
 
@@ -131,7 +130,7 @@
     count, span = u.shape
     return pl.pallas_call(
         prepare_kernel,
-        out_shape=jax.ShapeDtypeStruct((2 * span, count // 2), BF16),
+        out_shape=jax.ShapeDtypeStruct((2 * span, count), BF16),
         in_specs=[VMEM],
         out_specs=VMEM,
         compiler_params=pltpu.CompilerParams(vmem_limit_bytes=30 * MIB),
@@ -144,8 +143,7 @@
     if u_ref.dtype == BF16:
         u = u_ref[...]
     else:
-        start = pl.multiple_of(lax.rem(lax.axis_index("col"), 2) * width, width)
-        u = jnp.concatenate(split(u_ref[pl.ds(start, width), :].T), axis=0)
+        u = jnp.concatenate(split(u_ref[...].T), axis=0)
     row = lax.axis_index("row")
     code = jnp.int32(CODE[0])
     for r in range(1, 8):
@@ -218,7 +216,7 @@
         copy.wait()
 
 
-def final(x, mine, partner, chol, m, tile=1280):
+def final(x, mine, partner, chol, m, tile=640):
     count, width = x.shape[1], chol.shape[1]
     return pl.pallas_call(
         final_kernel,
@@ -239,14 +237,19 @@
     nchol, width = chol.shape
 
     keep, send = panel_pieces(pairs.reshape(16, 128), chol, slab_rows)
+    span = slab_columns.shape[0] // 2
+    core = lax.axis_index("col") % 2
+    there, here, send = lax.optimization_barrier(((1 - core) * span, core * span, send))
     pieces = keep + lax.ppermute(send, BOTH, CORE)
     own = jnp.sum(lax.all_to_all(pieces, "col", 0, 0, axis_index_groups=PLANE), axis=0)
     other = lax.ppermute(own, BOTH, ZPAIR)
     partner = lax.ppermute(own, BOTH, CORE)
 
-    theirs = mirror(own, other, prepare(after(slab_columns, own)), slab_columns.shape[0] // 2)
+    u = lax.dynamic_slice(after(slab_columns, own), (there, 0), (span, 128), allow_negative_indices=False)
+    theirs = mirror(own, other, prepare(u), span)
+    u = lax.dynamic_slice(after(slab_columns, theirs), (here, 0), (span, 128), allow_negative_indices=False)
     theirs = lax.ppermute(theirs, BOTH, CORE)
-    mine = mirror(own, other, slab_columns, slab_columns.shape[0] // 2)
+    mine = mirror(own, other, u, span)
     part = join(mine, theirs, own, other, partner)
     got = lax.all_to_all(part, "col", 0, 0, axis_index_groups=PLANE)
     x = got[:, :, width : width + 256].reshape(nchol, 256)

time: 109 us -> 108 us (level)
    unnamed x6, local copies, waits for them, and re-layouts: 3.6 us -> 0.02 us
    dynamic_slice x0 -> x2, local copies, waits for them, and re-layouts: none -> 2.59 us  [the longest x1 2.33 us: body(): lax.dynamic_slice(after(slab_columns, own), (there, 0), (span, 128), allo...]
  transfers between devices with their start and end apart: 6 -> 6, of which waited for: 3 -> 3; matrix products, arithmetic and copies ran while one was open for 0% -> 2% of each run, Pallas kernels for 2% -> 2%
where the time goes in v4:
time: 108 us
  blocking collectives  73.5 us (68%)
  Pallas kernels  13.1 us (12%)
  waiting for transfers between devices  12.6 us (12%)
  starting transfers between devices  5.03 us (5%)
  local copies, waits for them, and re-layouts  2.72 us (3%)
    all_to_all x1, blocking collectives, body(): mirrored = lax.all_to_all(spread, 'row', 0, 0).reshape(nchol, width)  29.7 us
    all_to_all x1, blocking collectives, body(): got = lax.all_to_all(part, 'col', 0, 0, axis_index_groups=PLANE)  27.8 us
    all_to_all x1, blocking collectives, body(): lax.all_to_all(pieces, 'col', 0, 0, axis_index_groups=PLANE)  15.9 us
    ppermute x1, waiting for transfers between devices, body(): turned = lax.ppermute(jnp.sum(got[:, :, :width], axis=0), BOTH, TURN)  9.38 us
    pallas_call x1, Pallas kernels, panel_pieces(): pl.pallas_call(panel_kernel, out_shape=[jax.ShapeDtypeStruct((8, nchol //...  6.95 us
    ppermute x1, starting transfers between devices, body(): turned = lax.ppermute(jnp.sum(got[:, :, :width], axis=0), BOTH, TURN)  3.26 us
    pallas_call x1, Pallas kernels, final(): pl.pallas_call(final_kernel, out_shape=jax.ShapeDtypeStruct((count, width...  3.24 us
    dynamic_slice x1, local copies, waits for them, and re-layouts, body(): lax.dynamic_slice(after(slab_columns, own), (there, 0), (span, 128), allo...  2.33 us
  transfers between devices with their start and end apart: 6, of which 3 were waited for; matrix products, arithmetic and copies ran while one was open for 2% of the time, Pallas kernels for 2%

profile of v4, /device:TPU:0, one launch (start us, length us, event | category | flops | bytes accessed | tf_op | source)
XLA Modules:
  0.0 108.1 jit_solution(6025940607168219639)
XLA Ops:
  0.0 7.0 %shard_map.46 = (f32[8,48,128]{2,1,0:T(8,128)}, f32[8,48,128]{2,1,0:T(8,128)}) custom-call(s32[16,128]{1,0:T(8,128)} %bitcast.9, f32[64,6400]{1,0:T(8,128)} %chol_ref.3, f32[256,6400]{1,0:T(8,128)} %rows_ref.1), custom_call_target="tpu_custom_call" | custom-call | tf_op jit(solution)/shard_map/pallas_call | solution.py:108
  7.0 0.1 collective-permute-start
  7.1 1.6 %collective-permute-done = f32[8,48,128]{2,1,0:T(8,128)S(1)} collective-permute-done((f32[8,48,128]{2,1,0:T(8,128)}, f32[8,48,128]{2,1,0:T(8,128)S(1)}, u32[]{:S(2)}, u32[]{:S(2)}) %collective-permute-start) | collective-permute-done | bytes 196640 | tf_op jit(solution)/shard_map/ppermute | solution.py:243
  8.7 1.0 add.8
  9.6 15.9 %all_to_all.15 = f32[8,48,128]{2,1,0:T(8,128)S(1)} all-to-all(f32[8,48,128]{2,1,0:T(8,128)S(1)} %add.8), channel_id=1, replica_groups={{0,2,4,6,8,10,12,14},{1,3,5,7,9,11,13,15},{16,18,20,22,24,26,28,30},{17..., dimensions={0} | all-to-all | bytes 393216 | tf_op jit(solution)/shard_map/all_to_all | solution.py:244
  25.6 1.1 %collective-permute-start.1 = (f32[48,128]{1,0:T(8,128)S(1)}, f32[48,128]{1,0:T(8,128)S(1)}, u32[]{:S(2)}, u32[]{:S(2)}) collective-permute-start(f32[48,128]{1,0:T(8,128)S(1)} %reduce_sum.18.own_ref), channel_id=1, source_target_pairs={{0,64},{1,65},{2,66},{3,67},{4,68},{5,69},{6,70},{7,71},{8,72},{9,... | collective-permute-start | bytes 73736 | tf_op jit(solution)/shard_map/ppermute | solution.py:245
  26.7 0.0 slice-start
  26.7 2.3 %constant_dynamic-slice_fusion.1.u_ref = f32[6400,128]{1,0:T(8,128)S(1)} fusion(f32[12800,128]{1,0:T(8,128)} %param.5, s32[]{:T(128)S(6)} %mul.6), kind=kLoop, calls=%fused_computation.4 | loop fusion | bytes 6553604 | tf_op jit(solution)/shard_map/dynamic_slice | solution.py:248
  29.0 0.0 slice-start.1
  29.0 0.9 shard_map.47.u_ref
  29.9 0.0 collective-permute-done.1.other_ref
  29.9 0.6 shard_map.48
  30.6 0.1 collective-permute-start.2
  30.6 0.5 collective-permute-start.3
  31.1 0.0 slice-done
  31.1 0.0 slice-done.1
  31.2 0.3 constant_dynamic-slice_fusion.u_ref
  31.4 1.1 %shard_map.49.mine_ref = f32[64,6400]{1,0:T(8,128)S(1)} custom-call(f32[48,128]{1,0:T(8,128)S(1)} %reduce_sum.18.own_ref, f32[48,128]{1,0:T(8,128)S(1)} %collective-permute-done.1.other_ref, f32[6400,128]{1,0:T(8,128)S(1)} %constant_dynamic-slice_fusion.u_ref), custom_call_target="tpu_custom_call" | custom-call | flops 314572800 | bytes 5242880 | tf_op jit(solution)/shard_map/pallas_call | solution.py:164
  32.6 1.6 %collective-permute-done.3.partner_ref = f32[48,128]{1,0:T(8,128)S(1)} collective-permute-done((f32[48,128]{1,0:T(8,128)S(1)}, f32[48,128]{1,0:T(8,128)S(1)}, u32[]{:S(2)}, u32[]{:S(2)}) %collective-permute-start.3) | collective-permute-done | bytes 24608 | tf_op jit(solution)/shard_map/ppermute | solution.py:246
  34.2 0.0 collective-permute-done.2.theirs_ref
  34.2 0.2 shard_map.50
  34.4 27.8 %all_to_all.16 = f32[8,8,6784]{2,1,0:T(8,128)S(1)} all-to-all(f32[8,8,6784]{2,1,0:T(8,128)S(1)} %shard_map.50), channel_id=1, replica_groups={{0,2,4,6,8,10,12,14},{1,3,5,7,9,11,13,15},{16,18,20,22,24,26,28,30},{17..., dimensions={0} | all-to-all | bytes 3473408 | tf_op jit(solution)/shard_map/all_to_all | solution.py:254
  62.2 0.0 collective-permute-start.4
  62.2 0.1 slice_reduce_fusion
  62.3 3.3 %collective-permute-start.5 = (f32[8,6400]{1,0:T(8,128)S(1)}, f32[8,6400]{1,0:T(8,128)S(1)}, u32[]{:S(2)}, u32[]{:S(2)}) collective-permute-start(f32[8,6400]{1,0:T(8,128)S(1)} %slice_reduce_fusion), channel_id=1, source_target_pairs={{0,32},{1,33},{2,64},{3,65},{4,0},{5,1},{6,80},{7,81},{8,16},{9,17... | collective-permute-start | bytes 614408 | tf_op jit(solution)/shard_map/ppermute | solution.py:258
  65.6 0.0 collective-permute-done.4.partner_ref
  65.6 9.4 %collective-permute-done.5 = f32[8,6400]{1,0:T(8,128)S(1)} collective-permute-done((f32[8,6400]{1,0:T(8,128)S(1)}, f32[8,6400]{1,0:T(8,128)S(1)}, u32[]{:S(2)}, u32[]{:S(2)}) %collective-permute-start.5) | collective-permute-done | bytes 204832 | tf_op jit(solution)/shard_map/ppermute | solution.py:258
  75.0 0.1 broadcast_in_dim.3
  75.1 0.0 copy-start
  75.1 29.7 %all_to_all.17 = f32[8,8,6400]{2,1,0:T(8,128)S(1)} all-to-all(f32[8,8,6400]{2,1,0:T(8,128)S(1)} %broadcast_in_dim.3), channel_id=1, replica_groups=mesh['row'=8,'col'=16] {'row'}, dimensions={0} | all-to-all | bytes 3276800 | tf_op jit(solution)/shard_map/all_to_all | solution.py:261
  104.8 0.0 copy-done
  104.8 3.2 %shard_map.51 = f32[256,6400]{1,0:T(8,128)} custom-call(f32[64,256]{1,0:T(8,128)S(1)} %slice_bitcast_fusion.x_ref, f32[64,128]{1,0:T(8,128)S(1)} %slice_bitcast_fusion.1.mine_ref, f32[64,128]{1,0:T(8,128)S(1)} %collective-permute-done.4.partner_ref, f32[64,6400]{1,0:T(8,128)S(1)} %copy-done, f32[64,6400]{1,0:T(8,128)S(1)} %bitcast.6), custom_call_target="tpu_custom_call" | custom-call | flops 1677721600 | bytes 10485760 | tf_op jit(solution)/shard_map/pallas_call | solution.py:221
  (4 shorter events, 0.0 us)
Async XLA Ops:
  7.0 1.7 %collective-permute-start = (f32[8,48,128]{2,1,0:T(8,128)}, f32[8,48,128]{2,1,0:T(8,128)S(1)}, u32[]{:S(2)}, u32[]{:S(2)}) collective-permute-start(f32[8,48,128]{2,1,0:T(8,128)} %get-tuple-element.15), channel_id=1, source_target_pairs={{0,1},{1,0},{2,3},{3,2},{4,5},{5,4},{6,7},{7,6},{8,9},{9,8},{10,11... | collective-permute-start | bytes 589832 | tf_op jit(solution)/shard_map/ppermute | solution.py:243
  25.6 4.4 %collective-permute-start.1 = (f32[48,128]{1,0:T(8,128)S(1)}, f32[48,128]{1,0:T(8,128)S(1)}, u32[]{:S(2)}, u32[]{:S(2)}) collective-permute-start(f32[48,128]{1,0:T(8,128)S(1)} %reduce_sum.18.own_ref), channel_id=1, source_target_pairs={{0,64},{1,65},{2,66},{3,67},{4,68},{5,69},{6,70},{7,71},{8,72},{9,... | collective-permute-start | bytes 73736 | tf_op jit(solution)/shard_map/ppermute | solution.py:245
  26.7 4.5 %slice-start = ((s8[6553600]{0:T(1024)(128)(4,1)}), s8[4194304]{0:T(1024)(128)(4,1)S(1)}, s32[]{:S(2)}) async-start(s8[6553600]{0:T(1024)(128)(4,1)} %bitcast.7), calls=%async_computation.3 | async-start | bytes 8388608
  29.0 2.1 %slice-start.1 = ((s8[6553600]{0:T(1024)(128)(4,1)}), s8[2359296]{0:T(1024)(128)(4,1)S(1)}, s32[]{:S(2)}) async-start(s8[6553600]{0:T(1024)(128)(4,1)} %bitcast.7), calls=%async_computation.4 | async-start | bytes 4718592
  30.6 3.6 %collective-permute-start.2 = (f32[64,6400]{1,0:T(8,128)S(1)}, f32[64,6400]{1,0:T(8,128)S(1)}, u32[]{:S(2)}, u32[]{:S(2)}) collective-permute-start(f32[64,6400]{1,0:T(8,128)S(1)} %shard_map.48), channel_id=1, source_target_pairs={{0,1},{1,0},{2,3},{3,2},{4,5},{5,4},{6,7},{7,6},{8,9},{9,8},{10,11... | collective-permute-start | bytes 4915208 | tf_op jit(solution)/shard_map/ppermute | solution.py:251
  30.6 3.5 %collective-permute-start.3 = (f32[48,128]{1,0:T(8,128)S(1)}, f32[48,128]{1,0:T(8,128)S(1)}, u32[]{:S(2)}, u32[]{:S(2)}) collective-permute-start(f32[48,128]{1,0:T(8,128)S(1)} %reduce_sum.18.own_ref), channel_id=1, source_target_pairs={{0,1},{1,0},{2,3},{3,2},{4,5},{5,4},{6,7},{7,6},{8,9},{9,8},{10,11... | collective-permute-start | bytes 73736 | tf_op jit(solution)/shard_map/ppermute | solution.py:246
  62.2 3.4 %collective-permute-start.4 = (f32[64,128]{1,0:T(8,128)S(1)}, f32[64,128]{1,0:T(8,128)S(1)}, u32[]{:S(2)}, u32[]{:S(2)}) collective-permute-start(f32[64,128]{1,0:T(8,128)S(1)} %slice_bitcast_fusion.1.mine_ref), channel_id=1, source_target_pairs={{0,1},{1,0},{2,3},{3,2},{4,5},{5,4},{6,7},{7,6},{8,9},{9,8},{10,11... | collective-permute-start | bytes 98312 | tf_op jit(solution)/shard_map/ppermute | solution.py:259
  62.3 12.7 %collective-permute-start.5 = (f32[8,6400]{1,0:T(8,128)S(1)}, f32[8,6400]{1,0:T(8,128)S(1)}, u32[]{:S(2)}, u32[]{:S(2)}) collective-permute-start(f32[8,6400]{1,0:T(8,128)S(1)} %slice_reduce_fusion), channel_id=1, source_target_pairs={{0,32},{1,33},{2,64},{3,65},{4,0},{5,1},{6,80},{7,81},{8,16},{9,17... | collective-permute-start | bytes 614408 | tf_op jit(solution)/shard_map/ppermute | solution.py:258
  75.1 29.8 %copy-start = (f32[64,6400]{1,0:T(8,128)S(1)}, f32[64,6400]{1,0:T(8,128)}, u32[]{:S(2)}) copy-start(f32[64,6400]{1,0:T(8,128)} %chol_ref.3) | copy-start | bytes 4915204

commit v5 on v4

--- a/solution.py
+++ b/solution.py
@@ -115,12 +115,11 @@
             pltpu.VMEM((steps, rows.shape[0], width // steps), F32),
             pltpu.SemaphoreType.DMA((steps + 1,)),
         ],
-        compiler_params=pltpu.CompilerParams(vmem_limit_bytes=57 * MIB),
+        compiler_params=pltpu.CompilerParams(vmem_limit_bytes=52 * MIB),
     )(pairs, chol, rows)
 
 
 def prepare_kernel(u_ref, out_ref):
-    width = out_ref.shape[1]
     hi, lo = split(u_ref[...].T)
     out_ref[:128, :] = hi
     out_ref[128:, :] = lo
@@ -138,12 +137,7 @@
     )(u)
 
 
-def mirror_kernel(own_ref, other_ref, u_ref, out_ref):
-    width = out_ref.shape[1]
-    if u_ref.dtype == BF16:
-        u = u_ref[...]
-    else:
-        u = jnp.concatenate(split(u_ref[...].T), axis=0)
+def panel_order(own_ref, other_ref):
     row = lax.axis_index("row")
     code = jnp.int32(CODE[0])
     for r in range(1, 8):
@@ -156,18 +150,55 @@
     hi, lo = split(jnp.concatenate(slices, axis=0))
     top = jnp.concatenate([hi, hi], axis=1)
     low = jnp.concatenate([lo, jnp.zeros_like(lo)], axis=1)
-    both = nn(jnp.concatenate([top, low], axis=0), u)
+    return jnp.concatenate([top, low], axis=0)
+
+
+def theirs_kernel(own_ref, other_ref, u_ref, out_ref):
+    both = nn(panel_order(own_ref, other_ref), u_ref[...])
     out_ref[...] = both[:64] + both[64:]
 
 
-def mirror(own, other, u, width):
-    return pl.pallas_call(
-        mirror_kernel,
-        out_shape=jax.ShapeDtypeStruct((64, width), F32),
+def theirs_part(own, other, u):
+    return pl.pallas_call(
+        theirs_kernel,
+        out_shape=jax.ShapeDtypeStruct((64, u.shape[1]), F32),
         in_specs=[VMEM] * 3,
         out_specs=VMEM,
         compiler_params=pltpu.CompilerParams(vmem_limit_bytes=30 * MIB),
-        cost_estimate=pl.CostEstimate(flops=6 * 64 * 128 * width, bytes_accessed=5 * MIB, transcendentals=0),
+    )(own, other, u)
+
+
+def mine_kernel(own_ref, other_ref, u_ref, out_ref, held, parts, sems):
+    steps, rows, span = held.shape
+    core = lax.rem(lax.axis_index("col"), 2)
+    loads = []
+    for k in range(steps):
+        start = pl.multiple_of(core * rows * steps + k * rows, rows)
+        loads.append(pltpu.make_async_copy(u_ref.at[pl.ds(start, rows), :], held.at[k], sems.at[k]))
+        loads[k].start()
+    for k in range(steps):
+        loads[k].wait()
+        hi, lo = split(held[k].T)
+        parts[:span, k * rows : k * rows + rows] = hi
+        parts[span:, k * rows : k * rows + rows] = lo
+    both = nn(panel_order(own_ref, other_ref), parts[...])
+    out_ref[...] = both[:64] + both[64:]
+
+
+def mine_part(own, other, u, steps=2):
+    count, span = u.shape
+    return pl.pallas_call(
+        mine_kernel,
+        out_shape=jax.ShapeDtypeStruct((64, count // 2), F32),
+        in_specs=[VMEM, VMEM, ANY],
+        out_specs=VMEM,
+        scratch_shapes=[
+            pltpu.VMEM((steps, count // 2 // steps, span), F32),
+            pltpu.VMEM((2 * span, count // 2), BF16),
+            pltpu.SemaphoreType.DMA((steps,)),
+        ],
+        compiler_params=pltpu.CompilerParams(vmem_limit_bytes=52 * MIB),
+        cost_estimate=pl.CostEstimate(flops=6 * 64 * span * count // 2, bytes_accessed=7 * MIB, transcendentals=0),
     )(own, other, u)
 
 
@@ -238,18 +269,16 @@
 
     keep, send = panel_pieces(pairs.reshape(16, 128), chol, slab_rows)
     span = slab_columns.shape[0] // 2
-    core = lax.axis_index("col") % 2
-    there, here, send = lax.optimization_barrier(((1 - core) * span, core * span, send))
+    there, send = lax.optimization_barrier(((1 - lax.axis_index("col") % 2) * span, send))
     pieces = keep + lax.ppermute(send, BOTH, CORE)
     own = jnp.sum(lax.all_to_all(pieces, "col", 0, 0, axis_index_groups=PLANE), axis=0)
     other = lax.ppermute(own, BOTH, ZPAIR)
     partner = lax.ppermute(own, BOTH, CORE)
 
     u = lax.dynamic_slice(after(slab_columns, own), (there, 0), (span, 128), allow_negative_indices=False)
-    theirs = mirror(own, other, prepare(u), span)
-    u = lax.dynamic_slice(after(slab_columns, theirs), (here, 0), (span, 128), allow_negative_indices=False)
+    theirs = theirs_part(own, other, prepare(u))
     theirs = lax.ppermute(theirs, BOTH, CORE)
-    mine = mirror(own, other, u, span)
+    mine = mine_part(own, other, slab_columns)
     part = join(mine, theirs, own, other, partner)
     got = lax.all_to_all(part, "col", 0, 0, axis_index_groups=PLANE)
     x = got[:, :, width : width + 256].reshape(nchol, 256)

time: 108 us -> 106 us (0.981)
  waiting for transfers between devices: 12.6 us -> 11.1 us
    pallas_call x2, Pallas kernels: 1.74 us -> 3.35 us  [the longest x1 2.75 us: mine_part(): pl.pallas_call(mine_kernel, out_shape=jax.ShapeDtypeStruct((64, count //...]
    pallas_call x1, Pallas kernels: 6.95 us -> 5.53 us  [panel_pieces(): pl.pallas_call(panel_kernel, out_shape=[jax.ShapeDtypeStruct((8, nchol //...]
    ppermute x1, waiting for transfers between devices: 1.61 us -> 0.27 us  [body(): partner = lax.ppermute(own, BOTH, CORE)]
  transfers between devices with their start and end apart: 6 -> 6, of which waited for: 3 -> 3; matrix products, arithmetic and copies ran while one was open for 2% -> 2% of each run, Pallas kernels for 2% -> 3%
where the time goes in v5:
time: 106 us
  blocking collectives  73.5 us (69%)
  Pallas kernels  13.2 us (12%)
  waiting for transfers between devices  11.1 us (10%)
  starting transfers between devices  5.03 us (5%)
  local copies, waits for them, and re-layouts  3 us (3%)
    all_to_all x1, blocking collectives, body(): mirrored = lax.all_to_all(spread, 'row', 0, 0).reshape(nchol, width)  29.8 us
    all_to_all x1, blocking collectives, body(): got = lax.all_to_all(part, 'col', 0, 0, axis_index_groups=PLANE)  27.8 us
    all_to_all x1, blocking collectives, body(): lax.all_to_all(pieces, 'col', 0, 0, axis_index_groups=PLANE)  15.9 us
    ppermute x1, waiting for transfers between devices, body(): turned = lax.ppermute(jnp.sum(got[:, :, :width], axis=0), BOTH, TURN)  9.38 us
    pallas_call x1, Pallas kernels, panel_pieces(): pl.pallas_call(panel_kernel, out_shape=[jax.ShapeDtypeStruct((8, nchol //...  5.53 us
    ppermute x1, starting transfers between devices, body(): turned = lax.ppermute(jnp.sum(got[:, :, :width], axis=0), BOTH, TURN)  3.26 us
    pallas_call x1, Pallas kernels, final(): pl.pallas_call(final_kernel, out_shape=jax.ShapeDtypeStruct((count, width...  3.24 us
    pallas_call x1, Pallas kernels, mine_part(): pl.pallas_call(mine_kernel, out_shape=jax.ShapeDtypeStruct((64, count //...  2.75 us
  transfers between devices with their start and end apart: 6, of which 3 were waited for; matrix products, arithmetic and copies ran while one was open for 2% of the time, Pallas kernels for 3%

profile of v5, /device:TPU:0, one launch (start us, length us, event | category | flops | bytes accessed | tf_op | source)
XLA Modules:
  0.0 106.1 jit_solution(7723797394429030734)
XLA Ops:
  0.0 0.0 copy-start.1
  0.0 0.7 copy-done.1
  0.7 5.5 %shard_map.46 = (f32[8,48,128]{2,1,0:T(8,128)S(1)}, f32[8,48,128]{2,1,0:T(8,128)S(1)}) custom-call(s32[16,128]{1,0:T(8,128)S(1)} %bitcast.7, f32[64,6400]{1,0:T(8,128)} %chol_ref.3, f32[256,6400]{1,0:T(8,128)} %rows_ref.1), custom_call_target="tpu_custom_call" | custom-call | tf_op jit(solution)/shard_map/pallas_call | solution.py:108
  6.2 0.1 collective-permute-start
  6.3 1.4 %collective-permute-done = f32[8,48,128]{2,1,0:T(8,128)S(1)} collective-permute-done((f32[8,48,128]{2,1,0:T(8,128)S(1)}, f32[8,48,128]{2,1,0:T(8,128)S(1)}, u32[]{:S(2)}, u32[]{:S(2)}) %collective-permute-start) | collective-permute-done | bytes 196640 | tf_op jit(solution)/shard_map/ppermute | solution.py:273
  7.8 15.9 %all_to_all.15 = f32[8,48,128]{2,1,0:T(8,128)S(1)} all-to-all(f32[8,48,128]{2,1,0:T(8,128)S(1)} %add.8), channel_id=1, replica_groups={{0,2,4,6,8,10,12,14},{1,3,5,7,9,11,13,15},{16,18,20,22,24,26,28,30},{17..., dimensions={0} | all-to-all | bytes 393216 | tf_op jit(solution)/shard_map/all_to_all | solution.py:274
  23.7 1.1 %collective-permute-start.1 = (f32[48,128]{1,0:T(8,128)S(1)}, f32[48,128]{1,0:T(8,128)S(1)}, u32[]{:S(2)}, u32[]{:S(2)}) collective-permute-start(f32[48,128]{1,0:T(8,128)S(1)} %reduce_sum.18.own_ref), channel_id=1, source_target_pairs={{0,64},{1,65},{2,66},{3,67},{4,68},{5,69},{6,70},{7,71},{8,72},{9,... | collective-permute-start | bytes 73736 | tf_op jit(solution)/shard_map/ppermute | solution.py:275
  24.8 2.2 %constant_dynamic-slice_fusion.u_ref = f32[6400,128]{1,0:T(8,128)S(1)} fusion(f32[12800,128]{1,0:T(8,128)} %u_ref.1, s32[]{:T(128)S(6)} %mul.3), kind=kLoop, calls=%fused_computation.3 | loop fusion | bytes 6553604 | tf_op jit(solution)/shard_map/dynamic_slice | solution.py:278
  27.0 0.9 shard_map.48.u_ref
  27.9 0.0 collective-permute-done.1.other_ref
  27.9 0.6 shard_map.49
  28.5 0.1 collective-permute-start.2
  28.6 0.5 collective-permute-start.3
  29.1 2.7 %shard_map.47.mine_ref = f32[64,6400]{1,0:T(8,128)S(1)} custom-call(f32[48,128]{1,0:T(8,128)S(1)} %reduce_sum.18.own_ref, f32[48,128]{1,0:T(8,128)S(1)} %collective-permute-done.1.other_ref, f32[12800,128]{1,0:T(8,128)} %u_ref.1), custom_call_target="tpu_custom_call" | custom-call | flops 314572800 | bytes 7340032 | tf_op jit(solution)/shard_map/pallas_call | solution.py:190
  31.9 0.3 collective-permute-done.3.partner_ref
  32.1 0.0 collective-permute-done.2.theirs_ref
  32.1 0.2 shard_map.50
  32.4 27.8 %all_to_all.16 = f32[8,8,6784]{2,1,0:T(8,128)S(1)} all-to-all(f32[8,8,6784]{2,1,0:T(8,128)S(1)} %shard_map.50), channel_id=1, replica_groups={{0,2,4,6,8,10,12,14},{1,3,5,7,9,11,13,15},{16,18,20,22,24,26,28,30},{17..., dimensions={0} | all-to-all | bytes 3473408 | tf_op jit(solution)/shard_map/all_to_all | solution.py:283
  60.2 0.0 collective-permute-start.4
  60.2 0.1 slice_reduce_fusion
  60.3 3.3 %collective-permute-start.5 = (f32[8,6400]{1,0:T(8,128)S(1)}, f32[8,6400]{1,0:T(8,128)S(1)}, u32[]{:S(2)}, u32[]{:S(2)}) collective-permute-start(f32[8,6400]{1,0:T(8,128)S(1)} %slice_reduce_fusion), channel_id=1, source_target_pairs={{0,32},{1,33},{2,64},{3,65},{4,0},{5,1},{6,80},{7,81},{8,16},{9,17... | collective-permute-start | bytes 614408 | tf_op jit(solution)/shard_map/ppermute | solution.py:287
  63.5 0.0 collective-permute-done.4.partner_ref
  63.6 9.4 %collective-permute-done.5 = f32[8,6400]{1,0:T(8,128)S(1)} collective-permute-done((f32[8,6400]{1,0:T(8,128)S(1)}, f32[8,6400]{1,0:T(8,128)S(1)}, u32[]{:S(2)}, u32[]{:S(2)}) %collective-permute-start.5) | collective-permute-done | bytes 204832 | tf_op jit(solution)/shard_map/ppermute | solution.py:287
  72.9 0.1 broadcast_in_dim.3
  73.0 0.0 copy-start
  73.1 29.8 %all_to_all.17 = f32[8,8,6400]{2,1,0:T(8,128)S(1)} all-to-all(f32[8,8,6400]{2,1,0:T(8,128)S(1)} %broadcast_in_dim.3), channel_id=1, replica_groups=mesh['row'=8,'col'=16] {'row'}, dimensions={0} | all-to-all | bytes 3276800 | tf_op jit(solution)/shard_map/all_to_all | solution.py:290
  102.8 0.0 copy-done
  102.8 3.2 %shard_map.51 = f32[256,6400]{1,0:T(8,128)} custom-call(f32[64,256]{1,0:T(8,128)S(1)} %slice_bitcast_fusion.x_ref, f32[64,128]{1,0:T(8,128)S(1)} %slice_bitcast_fusion.1.mine_ref, f32[64,128]{1,0:T(8,128)S(1)} %collective-permute-done.4.partner_ref, f32[64,6400]{1,0:T(8,128)S(1)} %copy-done, f32[64,6400]{1,0:T(8,128)S(1)} %bitcast.6), custom_call_target="tpu_custom_call" | custom-call | flops 1677721600 | bytes 10485760 | tf_op jit(solution)/shard_map/pallas_call | solution.py:252
  (4 shorter events, 0.0 us)
Async XLA Ops:
  0.0 0.7 copy-start.1
  6.2 1.5 %collective-permute-start = (f32[8,48,128]{2,1,0:T(8,128)S(1)}, f32[8,48,128]{2,1,0:T(8,128)S(1)}, u32[]{:S(2)}, u32[]{:S(2)}) collective-permute-start(f32[8,48,128]{2,1,0:T(8,128)S(1)} %get-tuple-element.13), channel_id=1, source_target_pairs={{0,1},{1,0},{2,3},{3,2},{4,5},{5,4},{6,7},{7,6},{8,9},{9,8},{10,11... | collective-permute-start | bytes 589832 | tf_op jit(solution)/shard_map/ppermute | solution.py:273
  23.7 4.2 %collective-permute-start.1 = (f32[48,128]{1,0:T(8,128)S(1)}, f32[48,128]{1,0:T(8,128)S(1)}, u32[]{:S(2)}, u32[]{:S(2)}) collective-permute-start(f32[48,128]{1,0:T(8,128)S(1)} %reduce_sum.18.own_ref), channel_id=1, source_target_pairs={{0,64},{1,65},{2,66},{3,67},{4,68},{5,69},{6,70},{7,71},{8,72},{9,... | collective-permute-start | bytes 73736 | tf_op jit(solution)/shard_map/ppermute | solution.py:275
  28.5 3.6 %collective-permute-start.2 = (f32[64,6400]{1,0:T(8,128)S(1)}, f32[64,6400]{1,0:T(8,128)S(1)}, u32[]{:S(2)}, u32[]{:S(2)}) collective-permute-start(f32[64,6400]{1,0:T(8,128)S(1)} %shard_map.49), channel_id=1, source_target_pairs={{0,1},{1,0},{2,3},{3,2},{4,5},{5,4},{6,7},{7,6},{8,9},{9,8},{10,11... | collective-permute-start | bytes 4915208 | tf_op jit(solution)/shard_map/ppermute | solution.py:280
  28.6 3.5 %collective-permute-start.3 = (f32[48,128]{1,0:T(8,128)S(1)}, f32[48,128]{1,0:T(8,128)S(1)}, u32[]{:S(2)}, u32[]{:S(2)}) collective-permute-start(f32[48,128]{1,0:T(8,128)S(1)} %reduce_sum.18.own_ref), channel_id=1, source_target_pairs={{0,1},{1,0},{2,3},{3,2},{4,5},{5,4},{6,7},{7,6},{8,9},{9,8},{10,11... | collective-permute-start | bytes 73736 | tf_op jit(solution)/shard_map/ppermute | solution.py:276
  60.2 3.3 %collective-permute-start.4 = (f32[64,128]{1,0:T(8,128)S(1)}, f32[64,128]{1,0:T(8,128)S(1)}, u32[]{:S(2)}, u32[]{:S(2)}) collective-permute-start(f32[64,128]{1,0:T(8,128)S(1)} %slice_bitcast_fusion.1.mine_ref), channel_id=1, source_target_pairs={{0,1},{1,0},{2,3},{3,2},{4,5},{5,4},{6,7},{7,6},{8,9},{9,8},{10,11... | collective-permute-start | bytes 98312 | tf_op jit(solution)/shard_map/ppermute | solution.py:288
  60.3 12.7 %collective-permute-start.5 = (f32[8,6400]{1,0:T(8,128)S(1)}, f32[8,6400]{1,0:T(8,128)S(1)}, u32[]{:S(2)}, u32[]{:S(2)}) collective-permute-start(f32[8,6400]{1,0:T(8,128)S(1)} %slice_reduce_fusion), channel_id=1, source_target_pairs={{0,32},{1,33},{2,64},{3,65},{4,0},{5,1},{6,80},{7,81},{8,16},{9,17... | collective-permute-start | bytes 614408 | tf_op jit(solution)/shard_map/ppermute | solution.py:287
  73.0 29.8 %copy-start = (f32[64,6400]{1,0:T(8,128)S(1)}, f32[64,6400]{1,0:T(8,128)}, u32[]{:S(2)}) copy-start(f32[64,6400]{1,0:T(8,128)} %chol_ref.3) | copy-start | bytes 4915204

commit v6 on v5

--- a/solution.py
+++ b/solution.py
@@ -119,20 +119,33 @@
     )(pairs, chol, rows)
 
 
-def prepare_kernel(u_ref, out_ref):
-    hi, lo = split(u_ref[...].T)
-    out_ref[:128, :] = hi
-    out_ref[128:, :] = lo
-
-
-def prepare(u):
+def fill(out_ref, u_ref, held, sems, core):
+    steps, rows, span = held.shape
+    loads = []
+    for k in range(steps):
+        start = pl.multiple_of(core * rows * steps + k * rows, rows)
+        loads.append(pltpu.make_async_copy(u_ref.at[pl.ds(start, rows), :], held.at[k], sems.at[k]))
+        loads[k].start()
+    for k in range(steps):
+        loads[k].wait()
+        hi, lo = split(held[k].T)
+        out_ref[:span, k * rows : k * rows + rows] = hi
+        out_ref[span:, k * rows : k * rows + rows] = lo
+
+
+def prepare_kernel(u_ref, out_ref, held, sems):
+    fill(out_ref, u_ref, held, sems, 1 - lax.rem(lax.axis_index("col"), 2))
+
+
+def prepare(u, steps=2):
     count, span = u.shape
     return pl.pallas_call(
         prepare_kernel,
-        out_shape=jax.ShapeDtypeStruct((2 * span, count), BF16),
-        in_specs=[VMEM],
+        out_shape=jax.ShapeDtypeStruct((2 * span, count // 2), BF16),
+        in_specs=[ANY],
         out_specs=VMEM,
-        compiler_params=pltpu.CompilerParams(vmem_limit_bytes=30 * MIB),
+        scratch_shapes=[pltpu.VMEM((steps, count // 2 // steps, span), F32), pltpu.SemaphoreType.DMA((steps,))],
+        compiler_params=pltpu.CompilerParams(vmem_limit_bytes=49 * MIB),
         cost_estimate=pl.CostEstimate(flops=0, bytes_accessed=7 * MIB, transcendentals=0),
     )(u)
 
@@ -202,39 +215,38 @@
     )(own, other, u)
 
 
-def join_kernel(mine_ref, theirs_ref, own_ref, other_ref, partner_ref, out_ref):
+def join_kernel(mine_ref, theirs_ref, own_ref, other_ref, out_ref):
     width = mine_ref.shape[1]
     half = own_ref.shape[0] - 16
-    col = lax.axis_index("col")
     out_ref[:, :, :width] = (mine_ref[...] + theirs_ref[...]).reshape(8, 8, width)
-    first = lax.rem(col, 2) == 0
-    mine, partner = own_ref[half + 8 :, :], partner_ref[half + 8 :, :]
     rows = slice(half, half + 8)
-    panel = jnp.where(col < 8, own_ref[rows, :], other_ref[rows, :])
-    extra = jnp.concatenate([jnp.where(first, mine, partner), jnp.where(first, partner, mine), panel], axis=1)
+    panel = jnp.where(lax.axis_index("col") < 8, own_ref[rows, :], other_ref[rows, :])
+    extra = jnp.concatenate([own_ref[half + 8 :, :], panel], axis=1)
     for j in range(8):
         out_ref[j, :, width:] = extra
 
 
-def join(mine, theirs, own, other, partner):
+def join(mine, theirs, own, other):
     return pl.pallas_call(
         join_kernel,
-        out_shape=jax.ShapeDtypeStruct((8, 8, mine.shape[1] + 384), F32),
-        in_specs=[VMEM] * 5,
+        out_shape=jax.ShapeDtypeStruct((8, 8, mine.shape[1] + 256), F32),
+        in_specs=[VMEM] * 4,
         out_specs=VMEM,
         compiler_params=pltpu.CompilerParams(vmem_limit_bytes=30 * MIB),
-    )(mine, theirs, own, other, partner)
-
-
-def final_kernel(x_ref, mine_ref, partner_ref, chol_ref, m_ref, out_ref, held, sems):
+    )(mine, theirs, own, other)
+
+
+def final_kernel(mine_ref, partner_ref, chol_ref, m_ref, out_ref, held, sems):
     tile = held.shape[2]
     half = mine_ref.shape[0] // 2
     first = lax.rem(lax.axis_index("col"), 2) == 0
-    rows = [jnp.where(first, mine_ref[...], partner_ref[...]), jnp.where(first, partner_ref[...], mine_ref[...])]
-    rows = jnp.concatenate(rows, axis=1)
+    mine, partner = mine_ref[...], partner_ref[...]
+    both = [jnp.where(first, mine, partner), jnp.where(first, partner, mine)]
+    x = jnp.concatenate([b[:, :128] for b in both], axis=1)
+    rows = jnp.concatenate([b[:, 128:] for b in both], axis=1)
     low = lax.axis_index("row") < 4
     rows = [jnp.where(low, rows[:half], rows[half:]), jnp.where(low, rows[half:], rows[:half])]
-    left = jnp.concatenate([x_ref[...], *rows], axis=0).T
+    left = jnp.concatenate([x, *rows], axis=0).T
     left = jnp.concatenate(split(left), axis=1)
     copies = []
     for k in range(held.shape[0]):
@@ -247,17 +259,17 @@
         copy.wait()
 
 
-def final(x, mine, partner, chol, m, tile=640):
-    count, width = x.shape[1], chol.shape[1]
+def final(mine, partner, chol, m, tile=640):
+    count, width = mine.shape[1], chol.shape[1]
     return pl.pallas_call(
         final_kernel,
         out_shape=jax.ShapeDtypeStruct((count, width), F32),
-        in_specs=[VMEM] * 5,
+        in_specs=[VMEM] * 4,
         out_specs=ANY,
         scratch_shapes=[pltpu.VMEM((width // tile, count, tile), F32), pltpu.SemaphoreType.DMA((width // tile,))],
         compiler_params=pltpu.CompilerParams(vmem_limit_bytes=30 * MIB),
         cost_estimate=pl.CostEstimate(flops=8 * count * 128 * width, bytes_accessed=10 * MIB, transcendentals=0),
-    )(x, mine, partner, chol, m)
+    )(mine, partner, chol, m)
 
 
 def after(x, *others):
@@ -268,27 +280,22 @@
     nchol, width = chol.shape
 
     keep, send = panel_pieces(pairs.reshape(16, 128), chol, slab_rows)
-    span = slab_columns.shape[0] // 2
-    there, send = lax.optimization_barrier(((1 - lax.axis_index("col") % 2) * span, send))
     pieces = keep + lax.ppermute(send, BOTH, CORE)
     own = jnp.sum(lax.all_to_all(pieces, "col", 0, 0, axis_index_groups=PLANE), axis=0)
     other = lax.ppermute(own, BOTH, ZPAIR)
-    partner = lax.ppermute(own, BOTH, CORE)
-
-    u = lax.dynamic_slice(after(slab_columns, own), (there, 0), (span, 128), allow_negative_indices=False)
-    theirs = theirs_part(own, other, prepare(u))
+
+    theirs = theirs_part(own, other, prepare(after(slab_columns, own)))
     theirs = lax.ppermute(theirs, BOTH, CORE)
     mine = mine_part(own, other, slab_columns)
-    part = join(mine, theirs, own, other, partner)
+    part = join(mine, theirs, own, other)
     got = lax.all_to_all(part, "col", 0, 0, axis_index_groups=PLANE)
-    x = got[:, :, width : width + 256].reshape(nchol, 256)
-    rows = got[:, :, width + 256 :].reshape(nchol, 128)
+    rest = got[:, :, width:].reshape(nchol, 256)
 
     turned = lax.ppermute(jnp.sum(got[:, :, :width], axis=0), BOTH, TURN)
-    partner = lax.ppermute(rows, BOTH, CORE)
-    spread = after(jnp.broadcast_to(turned, (8,) + turned.shape), x, rows, partner)
+    partner = lax.ppermute(rest, BOTH, CORE)
+    spread = after(jnp.broadcast_to(turned, (8,) + turned.shape), rest, partner)
     mirrored = lax.all_to_all(spread, "row", 0, 0).reshape(nchol, width)
-    return final(x, rows, partner, chol, mirrored)
+    return final(rest, partner, chol, mirrored)
 
 
 def solution(mesh):

time: 106 us -> 104 us (0.981)
  local copies, waits for them, and re-layouts: 3 us -> 0.81 us
  Pallas kernels: 13.2 us -> 14.8 us
  waiting for transfers between devices: 11.1 us -> 9.71 us
    ppermute x1, waiting for transfers between devices: 9.38 us -> 5.97 us  [body(): turned = lax.ppermute(jnp.sum(got[:, :, :width], axis=0), BOTH, TURN)]
    dynamic_slice x1 -> x0, local copies, waits for them, and re-layouts: 2.18 us -> none  [body(): lax.dynamic_slice(after(slab_columns, own), (there, 0), (span, 128), allo...]
    pallas_call x1, Pallas kernels: 0.91 us -> 2.47 us  [prepare(): pl.pallas_call(prepare_kernel, out_shape=jax.ShapeDtypeStruct((2 * span,...]
  transfers between devices with their start and end apart: 6 -> 5, of which waited for: 3 -> 5; matrix products, arithmetic and copies ran while one was open for 2% -> 0% of each run, Pallas kernels for 3% -> 5%
where the time goes in v6:
time: 104 us; the launch traced here: 103 us
  blocking collectives  73.4 us (71%)
  Pallas kernels  14.8 us (14%)
  waiting for transfers between devices  9.71 us (9%)
  starting transfers between devices  4.53 us (4%)
    all_to_all x1, blocking collectives, body(): mirrored = lax.all_to_all(spread, 'row', 0, 0).reshape(nchol, width)  30.3 us
    all_to_all x1, blocking collectives, body(): got = lax.all_to_all(part, 'col', 0, 0, axis_index_groups=PLANE)  27.2 us
    all_to_all x1, blocking collectives, body(): lax.all_to_all(pieces, 'col', 0, 0, axis_index_groups=PLANE)  15.9 us
    ppermute x1, waiting for transfers between devices, body(): turned = lax.ppermute(jnp.sum(got[:, :, :width], axis=0), BOTH, TURN)  5.97 us
    pallas_call x1, Pallas kernels, panel_pieces(): pl.pallas_call(panel_kernel, out_shape=[jax.ShapeDtypeStruct((8, nchol //...  5.53 us
    ppermute x1, starting transfers between devices, body(): turned = lax.ppermute(jnp.sum(got[:, :, :width], axis=0), BOTH, TURN)  3.26 us
    pallas_call x1, Pallas kernels, final(): pl.pallas_call(final_kernel, out_shape=jax.ShapeDtypeStruct((count, width...  3.25 us
    pallas_call x1, Pallas kernels, mine_part(): pl.pallas_call(mine_kernel, out_shape=jax.ShapeDtypeStruct((64, count //...  2.75 us
  transfers between devices with their start and end apart: 5, of which 5 were waited for; matrix products, arithmetic and copies ran while one was open for 0% of the time, Pallas kernels for 5%

profile of v6, /device:TPU:0, one launch (start us, length us, event | category | flops | bytes accessed | tf_op | source)
XLA Modules:
  0.0 103.4 jit_solution(4337363933678981872)
XLA Ops:
  0.0 0.0 copy-start.1
  0.0 0.7 copy-done.1
  0.7 5.5 %shard_map.46 = (f32[8,48,128]{2,1,0:T(8,128)S(1)}, f32[8,48,128]{2,1,0:T(8,128)S(1)}) custom-call(s32[16,128]{1,0:T(8,128)S(1)} %bitcast.5, f32[64,6400]{1,0:T(8,128)} %chol_ref.3, f32[256,6400]{1,0:T(8,128)} %rows_ref.1), custom_call_target="tpu_custom_call" | custom-call | tf_op jit(solution)/shard_map/pallas_call | solution.py:108
  6.2 0.1 collective-permute-start
  6.3 1.4 %collective-permute-done = f32[8,48,128]{2,1,0:T(8,128)S(1)} collective-permute-done((f32[8,48,128]{2,1,0:T(8,128)S(1)}, f32[8,48,128]{2,1,0:T(8,128)S(1)}, u32[]{:S(2)}, u32[]{:S(2)}) %collective-permute-start) | collective-permute-done | bytes 196640 | tf_op jit(solution)/shard_map/ppermute | solution.py:283
  7.8 15.9 %all_to_all.15 = f32[8,48,128]{2,1,0:T(8,128)S(1)} all-to-all(f32[8,48,128]{2,1,0:T(8,128)S(1)} %add.3), channel_id=1, replica_groups={{0,2,4,6,8,10,12,14},{1,3,5,7,9,11,13,15},{16,18,20,22,24,26,28,30},{17..., dimensions={0} | all-to-all | bytes 393216 | tf_op jit(solution)/shard_map/all_to_all | solution.py:284
  23.7 1.1 %collective-permute-start.1 = (f32[48,128]{1,0:T(8,128)S(1)}, f32[48,128]{1,0:T(8,128)S(1)}, u32[]{:S(2)}, u32[]{:S(2)}) collective-permute-start(f32[48,128]{1,0:T(8,128)S(1)} %reduce_sum.18.own_ref), channel_id=1, source_target_pairs={{0,64},{1,65},{2,66},{3,67},{4,68},{5,69},{6,70},{7,71},{8,72},{9,... | collective-permute-start | bytes 73736 | tf_op jit(solution)/shard_map/ppermute | solution.py:285
  24.8 2.5 %shard_map.48.u_ref = bf16[256,6400]{1,0:T(8,128)(2,1)S(1)} custom-call(f32[12800,128]{1,0:T(8,128)} %u_ref.2), custom_call_target="tpu_custom_call" | custom-call | bytes 7340032 | tf_op jit(solution)/shard_map/pallas_call | solution.py:142
  27.3 0.3 collective-permute-done.1.other_ref
  27.6 0.6 shard_map.49
  28.2 0.1 collective-permute-start.2
  28.3 2.8 %shard_map.47.mine_ref = f32[64,6400]{1,0:T(8,128)S(1)} custom-call(f32[48,128]{1,0:T(8,128)S(1)} %reduce_sum.18.own_ref, f32[48,128]{1,0:T(8,128)S(1)} %collective-permute-done.1.other_ref, f32[12800,128]{1,0:T(8,128)} %u_ref.2), custom_call_target="tpu_custom_call" | custom-call | flops 314572800 | bytes 7340032 | tf_op jit(solution)/shard_map/pallas_call | solution.py:203
  31.1 0.7 collective-permute-done.2.theirs_ref
  31.8 0.2 shard_map.50
  32.0 27.2 %all_to_all.16 = f32[8,8,6656]{2,1,0:T(8,128)S(1)} all-to-all(f32[8,8,6656]{2,1,0:T(8,128)S(1)} %shard_map.50), channel_id=1, replica_groups={{0,2,4,6,8,10,12,14},{1,3,5,7,9,11,13,15},{16,18,20,22,24,26,28,30},{17..., dimensions={0} | all-to-all | bytes 3407872 | tf_op jit(solution)/shard_map/all_to_all | solution.py:291
  59.2 0.1 slice_reduce_fusion
  59.3 3.3 %collective-permute-start.4 = (f32[8,6400]{1,0:T(8,128)S(1)}, f32[8,6400]{1,0:T(8,128)S(1)}, u32[]{:S(2)}, u32[]{:S(2)}) collective-permute-start(f32[8,6400]{1,0:T(8,128)S(1)} %slice_reduce_fusion), channel_id=1, source_target_pairs={{0,32},{1,33},{2,64},{3,65},{4,0},{5,1},{6,80},{7,81},{8,16},{9,17... | collective-permute-start | bytes 614408 | tf_op jit(solution)/shard_map/ppermute | solution.py:294
  62.5 0.0 collective-permute-start.3
  62.5 1.2 %collective-permute-done.3.partner_ref = f32[64,256]{1,0:T(8,128)S(1)} collective-permute-done((f32[64,256]{1,0:T(8,128)S(1)}, f32[64,256]{1,0:T(8,128)S(1)}, u32[]{:S(2)}, u32[]{:S(2)}) %collective-permute-start.3) | collective-permute-done | bytes 65568 | tf_op jit(solution)/shard_map/ppermute | solution.py:295
  63.8 6.0 %collective-permute-done.4 = f32[8,6400]{1,0:T(8,128)S(1)} collective-permute-done((f32[8,6400]{1,0:T(8,128)S(1)}, f32[8,6400]{1,0:T(8,128)S(1)}, u32[]{:S(2)}, u32[]{:S(2)}) %collective-permute-start.4) | collective-permute-done | bytes 204832 | tf_op jit(solution)/shard_map/ppermute | solution.py:294
  69.7 0.1 broadcast_in_dim.3
  69.9 0.0 copy-start
  69.9 30.3 %all_to_all.17 = f32[8,8,6400]{2,1,0:T(8,128)S(1)} all-to-all(f32[8,8,6400]{2,1,0:T(8,128)S(1)} %broadcast_in_dim.3), channel_id=1, replica_groups=mesh['row'=8,'col'=16] {'row'}, dimensions={0} | all-to-all | bytes 3276800 | tf_op jit(solution)/shard_map/all_to_all | solution.py:297
  100.1 0.0 copy-done
  100.1 3.3 %shard_map.51 = f32[256,6400]{1,0:T(8,128)} custom-call(f32[64,256]{1,0:T(8,128)S(1)} %slice_bitcast_fusion.mine_ref, f32[64,256]{1,0:T(8,128)S(1)} %collective-permute-done.3.partner_ref, f32[64,6400]{1,0:T(8,128)S(1)} %copy-done, f32[64,6400]{1,0:T(8,128)S(1)} %bitcast.4), custom_call_target="tpu_custom_call" | custom-call | flops 1677721600 | bytes 10485760 | tf_op jit(solution)/shard_map/pallas_call | solution.py:264
  (3 shorter events, 0.1 us)
Async XLA Ops:
  0.0 0.7 copy-start.1
  6.2 1.5 %collective-permute-start = (f32[8,48,128]{2,1,0:T(8,128)S(1)}, f32[8,48,128]{2,1,0:T(8,128)S(1)}, u32[]{:S(2)}, u32[]{:S(2)}) collective-permute-start(f32[8,48,128]{2,1,0:T(8,128)S(1)} %get-tuple-element.10), channel_id=1, source_target_pairs={{0,1},{1,0},{2,3},{3,2},{4,5},{5,4},{6,7},{7,6},{8,9},{9,8},{10,11... | collective-permute-start | bytes 589832 | tf_op jit(solution)/shard_map/ppermute | solution.py:283
  23.7 3.9 %collective-permute-start.1 = (f32[48,128]{1,0:T(8,128)S(1)}, f32[48,128]{1,0:T(8,128)S(1)}, u32[]{:S(2)}, u32[]{:S(2)}) collective-permute-start(f32[48,128]{1,0:T(8,128)S(1)} %reduce_sum.18.own_ref), channel_id=1, source_target_pairs={{0,64},{1,65},{2,66},{3,67},{4,68},{5,69},{6,70},{7,71},{8,72},{9,... | collective-permute-start | bytes 73736 | tf_op jit(solution)/shard_map/ppermute | solution.py:285
  28.2 3.6 %collective-permute-start.2 = (f32[64,6400]{1,0:T(8,128)S(1)}, f32[64,6400]{1,0:T(8,128)S(1)}, u32[]{:S(2)}, u32[]{:S(2)}) collective-permute-start(f32[64,6400]{1,0:T(8,128)S(1)} %shard_map.49), channel_id=1, source_target_pairs={{0,1},{1,0},{2,3},{3,2},{4,5},{5,4},{6,7},{7,6},{8,9},{9,8},{10,11... | collective-permute-start | bytes 4915208 | tf_op jit(solution)/shard_map/ppermute | solution.py:288
  59.3 10.5 %collective-permute-start.4 = (f32[8,6400]{1,0:T(8,128)S(1)}, f32[8,6400]{1,0:T(8,128)S(1)}, u32[]{:S(2)}, u32[]{:S(2)}) collective-permute-start(f32[8,6400]{1,0:T(8,128)S(1)} %slice_reduce_fusion), channel_id=1, source_target_pairs={{0,32},{1,33},{2,64},{3,65},{4,0},{5,1},{6,80},{7,81},{8,16},{9,17... | collective-permute-start | bytes 614408 | tf_op jit(solution)/shard_map/ppermute | solution.py:294
  62.5 1.3 %collective-permute-start.3 = (f32[64,256]{1,0:T(8,128)S(1)}, f32[64,256]{1,0:T(8,128)S(1)}, u32[]{:S(2)}, u32[]{:S(2)}) collective-permute-start(f32[64,256]{1,0:T(8,128)S(1)} %slice_bitcast_fusion.mine_ref), channel_id=1, source_target_pairs={{0,1},{1,0},{2,3},{3,2},{4,5},{5,4},{6,7},{7,6},{8,9},{9,8},{10,11... | collective-permute-start | bytes 196616 | tf_op jit(solution)/shard_map/ppermute | solution.py:295
  69.9 30.3 %copy-start = (f32[64,6400]{1,0:T(8,128)S(1)}, f32[64,6400]{1,0:T(8,128)}, u32[]{:S(2)}) copy-start(f32[64,6400]{1,0:T(8,128)} %chol_ref.3) | copy-start | bytes 4915204

commit v7 on v6

--- a/solution.py
+++ b/solution.py
@@ -52,12 +52,14 @@
     return lax.dot_general(a, b, (((1,), (0,)), ((), ())), preferred_element_type=F32)
 
 
-def panel_kernel(pairs_ref, chol_ref, rows_ref, keep_ref, send_ref, chol_held, rows_held, sems):
+def panel_kernel(pairs_any, chol_ref, rows_ref, keep_ref, send_ref, pairs_ref, chol_held, rows_held, sems):
     nchol, width = chol_held.shape
     half = nchol // 2
     tiles = width // 128
     steps = rows_held.shape[0]
     chunk = width // steps
+    load_pairs = pltpu.make_async_copy(pairs_any, pairs_ref, sems.at[steps + 1])
+    load_pairs.start()
     load_chol = pltpu.make_async_copy(chol_ref, chol_held, sems.at[steps])
     load_chol.start()
     loads = []
@@ -74,6 +76,7 @@
         keep_ref[j, where, :] = jnp.where(first, pair[:, :128], pair[:, 128:])
         send_ref[j, where, :] = jnp.where(first, pair[:, 128:], pair[:, :128])
 
+    load_pairs.wait()
     load_chol.wait()
     mine = chol_held.at[pl.ds(pl.multiple_of(row // 4 * half, half), half), :]
     stack = jnp.concatenate([mine[:, t * 128 : t * 128 + 128] for t in range(tiles)], axis=0)
@@ -108,12 +111,13 @@
     return pl.pallas_call(
         panel_kernel,
         out_shape=[jax.ShapeDtypeStruct((8, nchol // 2 + 16, 128), F32)] * 2,
-        in_specs=[VMEM, ANY, ANY],
+        in_specs=[ANY, ANY, ANY],
         out_specs=[VMEM, VMEM],
         scratch_shapes=[
+            pltpu.VMEM(pairs.shape, jnp.int32),
             pltpu.VMEM(chol.shape, F32),
             pltpu.VMEM((steps, rows.shape[0], width // steps), F32),
-            pltpu.SemaphoreType.DMA((steps + 1,)),
+            pltpu.SemaphoreType.DMA((steps + 2,)),
         ],
         compiler_params=pltpu.CompilerParams(vmem_limit_bytes=52 * MIB),
     )(pairs, chol, rows)
@@ -272,6 +276,10 @@
     )(mine, partner, chol, m)
 
 
+def far(x):
+    return pltpu.with_memory_space_constraint(x, pltpu.HBM)
+
+
 def after(x, *others):
     return lax.optimization_barrier((x, *others))[0]
 
@@ -279,7 +287,7 @@
 def body(slab_rows, slab_columns, chol, pairs):
     nchol, width = chol.shape
 
-    keep, send = panel_pieces(pairs.reshape(16, 128), chol, slab_rows)
+    keep, send = panel_pieces(far(pairs.reshape(16, 128)), far(chol), far(slab_rows))
     pieces = keep + lax.ppermute(send, BOTH, CORE)
     own = jnp.sum(lax.all_to_all(pieces, "col", 0, 0, axis_index_groups=PLANE), axis=0)
     other = lax.ppermute(own, BOTH, ZPAIR)

time: 104 us -> 103 us (level)
  no operation moved by 1% of the time
where the time goes in v7:
time: 103 us
  blocking collectives  73.4 us (71%)
  Pallas kernels  14.8 us (14%)
  waiting for transfers between devices  9.7 us (9%)
  starting transfers between devices  4.54 us (4%)
    all_to_all x1, blocking collectives, body(): mirrored = lax.all_to_all(spread, 'row', 0, 0).reshape(nchol, width)  30.3 us
    all_to_all x1, blocking collectives, body(): got = lax.all_to_all(part, 'col', 0, 0, axis_index_groups=PLANE)  27.2 us
    all_to_all x1, blocking collectives, body(): lax.all_to_all(pieces, 'col', 0, 0, axis_index_groups=PLANE)  15.9 us
    ppermute x1, waiting for transfers between devices, body(): turned = lax.ppermute(jnp.sum(got[:, :, :width], axis=0), BOTH, TURN)  5.97 us
    pallas_call x1, Pallas kernels, panel_pieces(): pl.pallas_call(panel_kernel, out_shape=[jax.ShapeDtypeStruct((8, nchol //...  5.56 us
    ppermute x1, starting transfers between devices, body(): turned = lax.ppermute(jnp.sum(got[:, :, :width], axis=0), BOTH, TURN)  3.27 us
    pallas_call x1, Pallas kernels, final(): pl.pallas_call(final_kernel, out_shape=jax.ShapeDtypeStruct((count, width...  3.25 us
    pallas_call x1, Pallas kernels, mine_part(): pl.pallas_call(mine_kernel, out_shape=jax.ShapeDtypeStruct((64, count //...  2.76 us
  transfers between devices with their start and end apart: 5, of which 5 were waited for; matrix products, arithmetic and copies ran while one was open for 0% of the time, Pallas kernels for 5%

profile of v7, /device:TPU:0, one launch (start us, length us, event | category | flops | bytes accessed | tf_op | source)
XLA Modules:
  0.0 102.7 jit_solution(10849953571642247963)
XLA Ops:
  0.0 5.6 %shard_map.46 = (f32[8,48,128]{2,1,0:T(8,128)S(1)}, f32[8,48,128]{2,1,0:T(8,128)S(1)}) custom-call(s32[16,128]{1,0:T(8,128)} %bitcast.5, f32[64,6400]{1,0:T(8,128)} %chol_ref.3, f32[256,6400]{1,0:T(8,128)} %rows_ref.1), custom_call_target="tpu_custom_call" | custom-call | tf_op jit(solution)/shard_map/pallas_call | solution.py:111
  5.6 0.1 collective-permute-start
  5.7 1.4 %collective-permute-done = f32[8,48,128]{2,1,0:T(8,128)S(1)} collective-permute-done((f32[8,48,128]{2,1,0:T(8,128)S(1)}, f32[8,48,128]{2,1,0:T(8,128)S(1)}, u32[]{:S(2)}, u32[]{:S(2)}) %collective-permute-start) | collective-permute-done | bytes 196640 | tf_op jit(solution)/shard_map/ppermute | solution.py:291
  7.1 15.9 %all_to_all.15 = f32[8,48,128]{2,1,0:T(8,128)S(1)} all-to-all(f32[8,48,128]{2,1,0:T(8,128)S(1)} %add.3), channel_id=1, replica_groups={{0,2,4,6,8,10,12,14},{1,3,5,7,9,11,13,15},{16,18,20,22,24,26,28,30},{17..., dimensions={0} | all-to-all | bytes 393216 | tf_op jit(solution)/shard_map/all_to_all | solution.py:292
  23.0 1.1 %collective-permute-start.1 = (f32[48,128]{1,0:T(8,128)S(1)}, f32[48,128]{1,0:T(8,128)S(1)}, u32[]{:S(2)}, u32[]{:S(2)}) collective-permute-start(f32[48,128]{1,0:T(8,128)S(1)} %reduce_sum.18.own_ref), channel_id=1, source_target_pairs={{0,64},{1,65},{2,66},{3,67},{4,68},{5,69},{6,70},{7,71},{8,72},{9,... | collective-permute-start | bytes 73736 | tf_op jit(solution)/shard_map/ppermute | solution.py:293
  24.1 2.5 %shard_map.48.u_ref = bf16[256,6400]{1,0:T(8,128)(2,1)S(1)} custom-call(f32[12800,128]{1,0:T(8,128)} %u_ref.2), custom_call_target="tpu_custom_call" | custom-call | bytes 7340032 | tf_op jit(solution)/shard_map/pallas_call | solution.py:146
  26.6 0.3 collective-permute-done.1.other_ref
  26.9 0.6 shard_map.49
  27.5 0.1 collective-permute-start.2
  27.6 2.8 %shard_map.47.mine_ref = f32[64,6400]{1,0:T(8,128)S(1)} custom-call(f32[48,128]{1,0:T(8,128)S(1)} %reduce_sum.18.own_ref, f32[48,128]{1,0:T(8,128)S(1)} %collective-permute-done.1.other_ref, f32[12800,128]{1,0:T(8,128)} %u_ref.2), custom_call_target="tpu_custom_call" | custom-call | flops 314572800 | bytes 7340032 | tf_op jit(solution)/shard_map/pallas_call | solution.py:207
  30.4 0.7 collective-permute-done.2.theirs_ref
  31.1 0.2 shard_map.50
  31.3 27.2 %all_to_all.16 = f32[8,8,6656]{2,1,0:T(8,128)S(1)} all-to-all(f32[8,8,6656]{2,1,0:T(8,128)S(1)} %shard_map.50), channel_id=1, replica_groups={{0,2,4,6,8,10,12,14},{1,3,5,7,9,11,13,15},{16,18,20,22,24,26,28,30},{17..., dimensions={0} | all-to-all | bytes 3407872 | tf_op jit(solution)/shard_map/all_to_all | solution.py:299
  58.5 0.1 slice_reduce_fusion
  58.6 3.3 %collective-permute-start.4 = (f32[8,6400]{1,0:T(8,128)S(1)}, f32[8,6400]{1,0:T(8,128)S(1)}, u32[]{:S(2)}, u32[]{:S(2)}) collective-permute-start(f32[8,6400]{1,0:T(8,128)S(1)} %slice_reduce_fusion), channel_id=1, source_target_pairs={{0,32},{1,33},{2,64},{3,65},{4,0},{5,1},{6,80},{7,81},{8,16},{9,17... | collective-permute-start | bytes 614408 | tf_op jit(solution)/shard_map/ppermute | solution.py:302
  61.9 0.0 collective-permute-start.3
  61.9 1.2 %collective-permute-done.3.partner_ref = f32[64,256]{1,0:T(8,128)S(1)} collective-permute-done((f32[64,256]{1,0:T(8,128)S(1)}, f32[64,256]{1,0:T(8,128)S(1)}, u32[]{:S(2)}, u32[]{:S(2)}) %collective-permute-start.3) | collective-permute-done | bytes 65568 | tf_op jit(solution)/shard_map/ppermute | solution.py:303
  63.1 6.0 %collective-permute-done.4 = f32[8,6400]{1,0:T(8,128)S(1)} collective-permute-done((f32[8,6400]{1,0:T(8,128)S(1)}, f32[8,6400]{1,0:T(8,128)S(1)}, u32[]{:S(2)}, u32[]{:S(2)}) %collective-permute-start.4) | collective-permute-done | bytes 204832 | tf_op jit(solution)/shard_map/ppermute | solution.py:302
  69.1 0.1 broadcast_in_dim.3
  69.2 0.0 copy-start
  69.2 30.3 %all_to_all.17 = f32[8,8,6400]{2,1,0:T(8,128)S(1)} all-to-all(f32[8,8,6400]{2,1,0:T(8,128)S(1)} %broadcast_in_dim.3), channel_id=1, replica_groups=mesh['row'=8,'col'=16] {'row'}, dimensions={0} | all-to-all | bytes 3276800 | tf_op jit(solution)/shard_map/all_to_all | solution.py:305
  99.5 0.0 copy-done
  99.5 3.3 %shard_map.51 = f32[256,6400]{1,0:T(8,128)} custom-call(f32[64,256]{1,0:T(8,128)S(1)} %slice_bitcast_fusion.mine_ref, f32[64,256]{1,0:T(8,128)S(1)} %collective-permute-done.3.partner_ref, f32[64,6400]{1,0:T(8,128)S(1)} %copy-done, f32[64,6400]{1,0:T(8,128)S(1)} %bitcast.4), custom_call_target="tpu_custom_call" | custom-call | flops 1677721600 | bytes 10485760 | tf_op jit(solution)/shard_map/pallas_call | solution.py:268
  (3 shorter events, 0.0 us)
Async XLA Ops:
  5.6 1.5 %collective-permute-start = (f32[8,48,128]{2,1,0:T(8,128)S(1)}, f32[8,48,128]{2,1,0:T(8,128)S(1)}, u32[]{:S(2)}, u32[]{:S(2)}) collective-permute-start(f32[8,48,128]{2,1,0:T(8,128)S(1)} %get-tuple-element.10), channel_id=1, source_target_pairs={{0,1},{1,0},{2,3},{3,2},{4,5},{5,4},{6,7},{7,6},{8,9},{9,8},{10,11... | collective-permute-start | bytes 589832 | tf_op jit(solution)/shard_map/ppermute | solution.py:291
  23.0 3.9 %collective-permute-start.1 = (f32[48,128]{1,0:T(8,128)S(1)}, f32[48,128]{1,0:T(8,128)S(1)}, u32[]{:S(2)}, u32[]{:S(2)}) collective-permute-start(f32[48,128]{1,0:T(8,128)S(1)} %reduce_sum.18.own_ref), channel_id=1, source_target_pairs={{0,64},{1,65},{2,66},{3,67},{4,68},{5,69},{6,70},{7,71},{8,72},{9,... | collective-permute-start | bytes 73736 | tf_op jit(solution)/shard_map/ppermute | solution.py:293
  27.5 3.6 %collective-permute-start.2 = (f32[64,6400]{1,0:T(8,128)S(1)}, f32[64,6400]{1,0:T(8,128)S(1)}, u32[]{:S(2)}, u32[]{:S(2)}) collective-permute-start(f32[64,6400]{1,0:T(8,128)S(1)} %shard_map.49), channel_id=1, source_target_pairs={{0,1},{1,0},{2,3},{3,2},{4,5},{5,4},{6,7},{7,6},{8,9},{9,8},{10,11... | collective-permute-start | bytes 4915208 | tf_op jit(solution)/shard_map/ppermute | solution.py:296
  58.6 10.5 %collective-permute-start.4 = (f32[8,6400]{1,0:T(8,128)S(1)}, f32[8,6400]{1,0:T(8,128)S(1)}, u32[]{:S(2)}, u32[]{:S(2)}) collective-permute-start(f32[8,6400]{1,0:T(8,128)S(1)} %slice_reduce_fusion), channel_id=1, source_target_pairs={{0,32},{1,33},{2,64},{3,65},{4,0},{5,1},{6,80},{7,81},{8,16},{9,17... | collective-permute-start | bytes 614408 | tf_op jit(solution)/shard_map/ppermute | solution.py:302
  61.9 1.3 %collective-permute-start.3 = (f32[64,256]{1,0:T(8,128)S(1)}, f32[64,256]{1,0:T(8,128)S(1)}, u32[]{:S(2)}, u32[]{:S(2)}) collective-permute-start(f32[64,256]{1,0:T(8,128)S(1)} %slice_bitcast_fusion.mine_ref), channel_id=1, source_target_pairs={{0,1},{1,0},{2,3},{3,2},{4,5},{5,4},{6,7},{7,6},{8,9},{9,8},{10,11... | collective-permute-start | bytes 196616 | tf_op jit(solution)/shard_map/ppermute | solution.py:303
  69.2 30.3 %copy-start = (f32[64,6400]{1,0:T(8,128)S(1)}, f32[64,6400]{1,0:T(8,128)}, u32[]{:S(2)}) copy-start(f32[64,6400]{1,0:T(8,128)} %chol_ref.3) | copy-start | bytes 4915204

commit v8 on v7

--- a/solution.py
+++ b/solution.py
@@ -81,7 +81,7 @@
     mine = chol_held.at[pl.ds(pl.multiple_of(row // 4 * half, half), half), :]
     stack = jnp.concatenate([mine[:, t * 128 : t * 128 + 128] for t in range(tiles)], axis=0)
     stack = jnp.concatenate(split(stack), axis=1)
-    for j in range(8):
+    def find(j):
         index = [pairs_ref[2 * j + i : 2 * j + i + 1, :] - col * width for i in range(2)]
         hot = jnp.concatenate([jnp.where(lanes == (i & 127), 1.0, 0.0) for i in index], axis=1).astype(BF16)
         found = nn(stack, jnp.concatenate([hot, hot], axis=0))
@@ -90,16 +90,20 @@
         for t in range(tiles):
             total = jnp.where(tile == t, found[t * half : t * half + half], total)
         put(j, slice(0, half), total)
+    for j in range(4):
+        find(j)
+    total = jnp.zeros((rows_held.shape[1], 2 * nchol), F32)
+    for k in range(steps):
+        loads[k].wait()
+        a = jnp.concatenate(split(chol_held[:, k * chunk : k * chunk + chunk]), axis=0)
+        b_hi, b_lo = split(rows_held[k])
+        total += nt(b_hi, a) + nt(b_lo, a)
+        for j in range(4 + 4 * k // steps, 4 + 4 * (k + 1) // steps):
+            find(j)
     for ref in (keep_ref, send_ref):
         for j in range(8):
             there = row if j < 4 else row ^ 4
             ref[j, half : half + 8, :] = ref[there, 8 * (j % 4) : 8 * (j % 4) + 8, :]
-    total = jnp.zeros((rows_held.shape[1], 2 * nchol), F32)
-    for k in range(steps):
-        loads[k].wait()
-        a = jnp.concatenate(split(chol_held[:, k * chunk : k * chunk + chunk]), axis=0)
-        b_hi, b_lo = split(rows_held[k])
-        total += nt(b_hi, a) + nt(b_lo, a)
     total = total.T
     x = total[:nchol] + total[nchol:]
     for j in range(8):

time: 103 us -> 103 us (level)
  no operation moved by 1% of the time
where the time goes in v8:
time: 103 us
  blocking collectives  73.3 us (71%)
  Pallas kernels  14.7 us (14%)
  waiting for transfers between devices  9.72 us (9%)
  starting transfers between devices  4.53 us (4%)
    all_to_all x1, blocking collectives, body(): mirrored = lax.all_to_all(spread, 'row', 0, 0).reshape(nchol, width)  30.3 us
    all_to_all x1, blocking collectives, body(): got = lax.all_to_all(part, 'col', 0, 0, axis_index_groups=PLANE)  27.2 us
    all_to_all x1, blocking collectives, body(): lax.all_to_all(pieces, 'col', 0, 0, axis_index_groups=PLANE)  15.9 us
    ppermute x1, waiting for transfers between devices, body(): turned = lax.ppermute(jnp.sum(got[:, :, :width], axis=0), BOTH, TURN)  5.97 us
    pallas_call x1, Pallas kernels, panel_pieces(): pl.pallas_call(panel_kernel, out_shape=[jax.ShapeDtypeStruct((8, nchol //...  5.48 us
    ppermute x1, starting transfers between devices, body(): turned = lax.ppermute(jnp.sum(got[:, :, :width], axis=0), BOTH, TURN)  3.27 us
    pallas_call x1, Pallas kernels, final(): pl.pallas_call(final_kernel, out_shape=jax.ShapeDtypeStruct((count, width...  3.25 us
    pallas_call x1, Pallas kernels, mine_part(): pl.pallas_call(mine_kernel, out_shape=jax.ShapeDtypeStruct((64, count //...  2.75 us
  transfers between devices with their start and end apart: 5, of which 5 were waited for; matrix products, arithmetic and copies ran while one was open for 0% of the time, Pallas kernels for 5%

profile of v8, /device:TPU:0, one launch (start us, length us, event | category | flops | bytes accessed | tf_op | source)
XLA Modules:
  0.0 102.6 jit_solution(18099209294014174310)
XLA Ops:
  0.0 5.5 %shard_map.46 = (f32[8,48,128]{2,1,0:T(8,128)S(1)}, f32[8,48,128]{2,1,0:T(8,128)S(1)}) custom-call(s32[16,128]{1,0:T(8,128)} %bitcast.5, f32[64,6400]{1,0:T(8,128)} %chol_ref.3, f32[256,6400]{1,0:T(8,128)} %rows_ref.1), custom_call_target="tpu_custom_call" | custom-call | tf_op jit(solution)/shard_map/pallas_call | solution.py:115
  5.5 0.1 collective-permute-start
  5.6 1.4 %collective-permute-done = f32[8,48,128]{2,1,0:T(8,128)S(1)} collective-permute-done((f32[8,48,128]{2,1,0:T(8,128)S(1)}, f32[8,48,128]{2,1,0:T(8,128)S(1)}, u32[]{:S(2)}, u32[]{:S(2)}) %collective-permute-start) | collective-permute-done | bytes 196640 | tf_op jit(solution)/shard_map/ppermute | solution.py:295
  7.0 15.9 %all_to_all.15 = f32[8,48,128]{2,1,0:T(8,128)S(1)} all-to-all(f32[8,48,128]{2,1,0:T(8,128)S(1)} %add.3), channel_id=1, replica_groups={{0,2,4,6,8,10,12,14},{1,3,5,7,9,11,13,15},{16,18,20,22,24,26,28,30},{17..., dimensions={0} | all-to-all | bytes 393216 | tf_op jit(solution)/shard_map/all_to_all | solution.py:296
  23.0 1.1 %collective-permute-start.1 = (f32[48,128]{1,0:T(8,128)S(1)}, f32[48,128]{1,0:T(8,128)S(1)}, u32[]{:S(2)}, u32[]{:S(2)}) collective-permute-start(f32[48,128]{1,0:T(8,128)S(1)} %reduce_sum.18.own_ref), channel_id=1, source_target_pairs={{0,64},{1,65},{2,66},{3,67},{4,68},{5,69},{6,70},{7,71},{8,72},{9,... | collective-permute-start | bytes 73736 | tf_op jit(solution)/shard_map/ppermute | solution.py:297
  24.0 2.5 %shard_map.48.u_ref = bf16[256,6400]{1,0:T(8,128)(2,1)S(1)} custom-call(f32[12800,128]{1,0:T(8,128)} %u_ref.2), custom_call_target="tpu_custom_call" | custom-call | bytes 7340032 | tf_op jit(solution)/shard_map/pallas_call | solution.py:150
  26.5 0.3 collective-permute-done.1.other_ref
  26.9 0.6 shard_map.49
  27.5 0.1 collective-permute-start.2
  27.6 2.8 %shard_map.47.mine_ref = f32[64,6400]{1,0:T(8,128)S(1)} custom-call(f32[48,128]{1,0:T(8,128)S(1)} %reduce_sum.18.own_ref, f32[48,128]{1,0:T(8,128)S(1)} %collective-permute-done.1.other_ref, f32[12800,128]{1,0:T(8,128)} %u_ref.2), custom_call_target="tpu_custom_call" | custom-call | flops 314572800 | bytes 7340032 | tf_op jit(solution)/shard_map/pallas_call | solution.py:211
  30.3 0.7 collective-permute-done.2.theirs_ref
  31.1 0.2 shard_map.50
  31.2 27.2 %all_to_all.16 = f32[8,8,6656]{2,1,0:T(8,128)S(1)} all-to-all(f32[8,8,6656]{2,1,0:T(8,128)S(1)} %shard_map.50), channel_id=1, replica_groups={{0,2,4,6,8,10,12,14},{1,3,5,7,9,11,13,15},{16,18,20,22,24,26,28,30},{17..., dimensions={0} | all-to-all | bytes 3407872 | tf_op jit(solution)/shard_map/all_to_all | solution.py:303
  58.4 0.1 slice_reduce_fusion
  58.5 3.3 %collective-permute-start.4 = (f32[8,6400]{1,0:T(8,128)S(1)}, f32[8,6400]{1,0:T(8,128)S(1)}, u32[]{:S(2)}, u32[]{:S(2)}) collective-permute-start(f32[8,6400]{1,0:T(8,128)S(1)} %slice_reduce_fusion), channel_id=1, source_target_pairs={{0,32},{1,33},{2,64},{3,65},{4,0},{5,1},{6,80},{7,81},{8,16},{9,17... | collective-permute-start | bytes 614408 | tf_op jit(solution)/shard_map/ppermute | solution.py:306
  61.8 0.0 collective-permute-start.3
  61.8 1.2 %collective-permute-done.3.partner_ref = f32[64,256]{1,0:T(8,128)S(1)} collective-permute-done((f32[64,256]{1,0:T(8,128)S(1)}, f32[64,256]{1,0:T(8,128)S(1)}, u32[]{:S(2)}, u32[]{:S(2)}) %collective-permute-start.3) | collective-permute-done | bytes 65568 | tf_op jit(solution)/shard_map/ppermute | solution.py:307
  63.0 6.0 %collective-permute-done.4 = f32[8,6400]{1,0:T(8,128)S(1)} collective-permute-done((f32[8,6400]{1,0:T(8,128)S(1)}, f32[8,6400]{1,0:T(8,128)S(1)}, u32[]{:S(2)}, u32[]{:S(2)}) %collective-permute-start.4) | collective-permute-done | bytes 204832 | tf_op jit(solution)/shard_map/ppermute | solution.py:306
  69.0 0.1 broadcast_in_dim.3
  69.1 0.0 copy-start
  69.1 30.3 %all_to_all.17 = f32[8,8,6400]{2,1,0:T(8,128)S(1)} all-to-all(f32[8,8,6400]{2,1,0:T(8,128)S(1)} %broadcast_in_dim.3), channel_id=1, replica_groups=mesh['row'=8,'col'=16] {'row'}, dimensions={0} | all-to-all | bytes 3276800 | tf_op jit(solution)/shard_map/all_to_all | solution.py:309
  99.4 0.0 copy-done
  99.4 3.3 %shard_map.51 = f32[256,6400]{1,0:T(8,128)} custom-call(f32[64,256]{1,0:T(8,128)S(1)} %slice_bitcast_fusion.mine_ref, f32[64,256]{1,0:T(8,128)S(1)} %collective-permute-done.3.partner_ref, f32[64,6400]{1,0:T(8,128)S(1)} %copy-done, f32[64,6400]{1,0:T(8,128)S(1)} %bitcast.4), custom_call_target="tpu_custom_call" | custom-call | flops 1677721600 | bytes 10485760 | tf_op jit(solution)/shard_map/pallas_call | solution.py:272
  (3 shorter events, 0.0 us)
Async XLA Ops:
  5.5 1.5 %collective-permute-start = (f32[8,48,128]{2,1,0:T(8,128)S(1)}, f32[8,48,128]{2,1,0:T(8,128)S(1)}, u32[]{:S(2)}, u32[]{:S(2)}) collective-permute-start(f32[8,48,128]{2,1,0:T(8,128)S(1)} %get-tuple-element.10), channel_id=1, source_target_pairs={{0,1},{1,0},{2,3},{3,2},{4,5},{5,4},{6,7},{7,6},{8,9},{9,8},{10,11... | collective-permute-start | bytes 589832 | tf_op jit(solution)/shard_map/ppermute | solution.py:295
  23.0 3.9 %collective-permute-start.1 = (f32[48,128]{1,0:T(8,128)S(1)}, f32[48,128]{1,0:T(8,128)S(1)}, u32[]{:S(2)}, u32[]{:S(2)}) collective-permute-start(f32[48,128]{1,0:T(8,128)S(1)} %reduce_sum.18.own_ref), channel_id=1, source_target_pairs={{0,64},{1,65},{2,66},{3,67},{4,68},{5,69},{6,70},{7,71},{8,72},{9,... | collective-permute-start | bytes 73736 | tf_op jit(solution)/shard_map/ppermute | solution.py:297
  27.5 3.6 %collective-permute-start.2 = (f32[64,6400]{1,0:T(8,128)S(1)}, f32[64,6400]{1,0:T(8,128)S(1)}, u32[]{:S(2)}, u32[]{:S(2)}) collective-permute-start(f32[64,6400]{1,0:T(8,128)S(1)} %shard_map.49), channel_id=1, source_target_pairs={{0,1},{1,0},{2,3},{3,2},{4,5},{5,4},{6,7},{7,6},{8,9},{9,8},{10,11... | collective-permute-start | bytes 4915208 | tf_op jit(solution)/shard_map/ppermute | solution.py:300
  58.5 10.5 %collective-permute-start.4 = (f32[8,6400]{1,0:T(8,128)S(1)}, f32[8,6400]{1,0:T(8,128)S(1)}, u32[]{:S(2)}, u32[]{:S(2)}) collective-permute-start(f32[8,6400]{1,0:T(8,128)S(1)} %slice_reduce_fusion), channel_id=1, source_target_pairs={{0,32},{1,33},{2,64},{3,65},{4,0},{5,1},{6,80},{7,81},{8,16},{9,17... | collective-permute-start | bytes 614408 | tf_op jit(solution)/shard_map/ppermute | solution.py:306
  61.8 1.3 %collective-permute-start.3 = (f32[64,256]{1,0:T(8,128)S(1)}, f32[64,256]{1,0:T(8,128)S(1)}, u32[]{:S(2)}, u32[]{:S(2)}) collective-permute-start(f32[64,256]{1,0:T(8,128)S(1)} %slice_bitcast_fusion.mine_ref), channel_id=1, source_target_pairs={{0,1},{1,0},{2,3},{3,2},{4,5},{5,4},{6,7},{7,6},{8,9},{9,8},{10,11... | collective-permute-start | bytes 196616 | tf_op jit(solution)/shard_map/ppermute | solution.py:307
  69.1 30.3 %copy-start = (f32[64,6400]{1,0:T(8,128)S(1)}, f32[64,6400]{1,0:T(8,128)}, u32[]{:S(2)}) copy-start(f32[64,6400]{1,0:T(8,128)} %chol_ref.3) | copy-start | bytes 4915204
